TPU v7x, 512 devices: a whole 4x4x16 slice. The times are simulated.
512 devices in a mesh: worker: 16 (over z), fsdp: 16 (over y_lo, x, core), tensor: 2 (over y_hi).
Axes of the slice: x: 4, y: 4 (y_hi: 2, y_lo: 2; y = y_hi * 2 + y_lo), z: 16, core: 2. Of those that a mesh axis runs over, the one named last changes fastest.
Arguments:
- token_ids: int32 [16, 4096], P('worker', 'fsdp'), may hold values from 0 to 128255, as said below
- features_in: bfloat16 [16, 4096, 8192], P('worker', 'fsdp', 'tensor')
- targets: bfloat16 [16, 4096, 512], P('worker', 'fsdp', 'tensor'), may hold values from -6 to 6
- local_weight: bfloat16 [16, 8192, 512], P('worker', 'fsdp', 'tensor'), may hold values from -0.0625 to 0.0625
- adam_first: bfloat16 [16, 8192, 512], P('worker', 'fsdp', 'tensor'), may hold values from -0.00390625 to 0.00390625
- adam_second: bfloat16 [16, 8192, 512], P('worker', 'fsdp', 'tensor'), may hold values from 9.95351e-09 to 9.983778e-07
- prev_delta: bfloat16 [16, 8192, 512], P('worker', 'fsdp', 'tensor'), may hold values from -0.046875 to 0.046875
- global_weight: bfloat16 [8192, 512], P('fsdp', 'tensor'), may hold values from -0.0625 to 0.0625
- outer_momentum: bfloat16 [8192, 512], P('fsdp', 'tensor'), may hold values from -0.046875 to 0.046875
- fragment_of_tile: int32 [64, 4], P('fsdp'), may hold values from 0 to 1, as said below
Outputs:
- new_local: bfloat16 [16, 8192, 512], P('worker', 'fsdp', 'tensor')
- new_first: bfloat16 [16, 8192, 512], P('worker', 'fsdp', 'tensor')
- new_second: bfloat16 [16, 8192, 512], P('worker', 'fsdp', 'tensor')
- new_global: bfloat16 [8192, 512], P('fsdp', 'tensor')
- new_momentum: bfloat16 [8192, 512], P('fsdp', 'tensor')
Inputs may be any that keep to these rules, and one draw needn't show every extreme that they name: `token_ids`: 0 marks padding; in each replica's row the first 1024 tokens or more are not padding, and padding only follows the last non-padding token. `fragment_of_tile`: every row of tiles holds 2 tiles of each of the 2 rounds.
All inputs are finite; a program needn't handle non-finite values.
Results may differ from a plain program's by a relative error of at most 0.02.
Values may be sent and summed in bfloat16 or wider, within the bound.
No kernel may reach another device: no remote copies, remote signals or barrier semaphores. Data moves between devices by JAX's collectives and lax.ppermute only.
A program may use at most 64 MiB of HBM per device.

v0:
```python
import jax
import jax.numpy as jnp
from jax import lax
from jax.sharding import PartitionSpec as P

HD = 128


def outer_update(delta_sum, momentum_old, global_old, replicas):
    outer_grad = delta_sum / replicas
    momentum = 0.9 * momentum_old.astype(jnp.float32) + outer_grad
    merged = global_old.astype(jnp.float32) - 0.7 * (outer_grad + 0.9 * momentum)
    return (momentum.astype(jnp.bfloat16), merged.astype(jnp.bfloat16))


def local(
    token_ids,
    features_in,
    targets,
    local_weight,
    adam_first,
    adam_second,
    prev_delta,
    global_weight,
    outer_momentum,
    fragment_of_tile,
):
    ids = token_ids[0]
    weight = local_weight[0]
    cols_here = weight.shape[1]
    whole = lax.all_gather(features_in[0], "tensor", axis=1, tiled=True)
    values = whole.astype(jnp.float32)
    inv = lax.rsqrt(jnp.mean(values * values, axis=1, keepdims=True) + 1e-05)
    normed = (values * inv).astype(jnp.bfloat16)
    mask = (ids != 0).astype(jnp.float32)
    columns = normed
    keys = jnp.dot(
        columns,
        lax.all_gather(weight, "fsdp", axis=0, tiled=True),
        preferred_element_type=jnp.float32,
    )
    resid = ((keys - targets[0].astype(jnp.float32)) * mask[:, None]).astype(jnp.bfloat16)
    columns = normed
    raw = lax.psum_scatter(
        lax.dot_general(
            columns, resid, (((0,), (0,)), ((), ())), preferred_element_type=jnp.float32
        ).astype(jnp.bfloat16),
        "fsdp",
        scatter_dimension=0,
        tiled=True,
    ).astype(jnp.float32)
    norm = jnp.sqrt(lax.psum(jnp.sum(raw * raw), ("fsdp", "tensor")))
    clipped = raw * jnp.minimum(1.0, 1.0 / (norm + 1e-06))
    first = 0.9 * adam_first[0].astype(jnp.float32) + 0.1 * clipped
    second = 0.95 * adam_second[0].astype(jnp.float32) + 0.05 * clipped * clipped
    old = weight.astype(jnp.float32)
    stepped = old - 0.0004 * (first / (jnp.sqrt(second) + 1e-08) + 0.1 * old)
    replicas = lax.axis_size("worker")
    delta = prev_delta[0].astype(jnp.float32)
    delta_sum = lax.psum(delta.astype(jnp.bfloat16), "worker").astype(jnp.float32)
    momentum_new, merged_new = outer_update(delta_sum, outer_momentum, global_weight, replicas)
    heads_here = cols_here // HD
    first_head = lax.axis_index("tensor") * heads_here
    tiles = lax.dynamic_slice_in_dim(fragment_of_tile, first_head, heads_here, 1)
    selected = jnp.repeat(jnp.repeat(tiles == 0, HD, axis=0), HD, axis=1)
    new_momentum = jnp.where(selected, momentum_new, outer_momentum)
    new_global = jnp.where(selected, merged_new, global_weight)
    mixed = 0.5 * stepped + 0.5 * new_global.astype(jnp.float32)
    new_local = jnp.where(selected, mixed, stepped).astype(jnp.bfloat16)
    return (
        new_local[None],
        first.astype(jnp.bfloat16)[None],
        second.astype(jnp.bfloat16)[None],
        new_global,
        new_momentum,
    )


def solution(mesh):
    placed = (
        P("worker", "fsdp"),
        P("worker", "fsdp", "tensor"),
        P("worker", "fsdp", "tensor"),
        P("worker", "fsdp", "tensor"),
        P("worker", "fsdp", "tensor"),
        P("worker", "fsdp", "tensor"),
        P("worker", "fsdp", "tensor"),
        P("fsdp", "tensor"),
        P("fsdp", "tensor"),
        P("fsdp", None),
    )
    return jax.shard_map(
        local,
        mesh=mesh,
        in_specs=placed,
        out_specs=(
            P("worker", "fsdp", "tensor"),
            P("worker", "fsdp", "tensor"),
            P("worker", "fsdp", "tensor"),
            P("fsdp", "tensor"),
            P("fsdp", "tensor"),
        ),
        check_vma=False,
    )
```

profile of v0, /device:TPU:1, one launch (start us, length us, event | category | flops | bytes accessed | tf_op | source)
XLA Modules:
  0.0 356.6 jit_solution(11727175055206743267)
XLA Ops:
  8.0 0.0 copy-start.7
  8.0 0.0 all-gather.5.cloned.1.call-start
  8.1 0.7 all-gather.5.cloned.1.call-update
  8.7 0.0 all-gather.7.cloned.1.call-start
  8.8 0.7 all-gather.7.cloned.1.call-update
  9.5 0.0 reduce-scatter.2.cloned.1.call-start
  9.5 0.7 compare_convert_fusion
  10.2 74.5 %all-gather.5.cloned.1.call-done = bf16[1,256,8192]{2,1,0:T(8,128)(2,1)} async-done(((bf16[1,256,4096]{2,1,0:T(8,128)(2,1)}), bf16[1,256,8192]{2,1,0:T(8,128)(2,1)}) %all-gather.5.cloned.1.call-update) | async-done | bytes 4194320 | tf_op jit(solution)/shard_map/all_gather | solution.py:31
  84.8 3.1 fusion
  87.9 43.9 %all-gather.7.cloned.1.call-done = bf16[1,8192,256]{2,1,0:T(8,128)(2,1)} async-done(((bf16[1,512,256]{2,1,0:T(8,128)(2,1)}), bf16[1,8192,256]{2,1,0:T(8,128)(2,1)}) %all-gather.7.cloned.1.call-update) | async-done | bytes 4194320 | tf_op jit(solution)/shard_map/all_gather | solution.py:39
  131.8 0.0 copy-done.7
  131.8 4.9 %fusion.16 = bf16[256,256]{1,0:T(8,128)(2,1)S(1)} fusion(bf16[1,8192,256]{2,1,0:T(8,128)(2,1)} %all-gather.7.cloned.1.call-done, bf16[1,256,8192]{2,1,0:T(8,128)(2,1)} %all-gather.5.cloned.1.call-done, f32[256]{0:T(256)S(1)} %add_rsqrt_fusion, bf16[1,256,256]{2,1,0:T(8,128)(2,1)S(1)} %copy-done.7, f32[256]{0:T(256)S(1)} %bitcast.69), kind=kOutput, calls=%fused_computation.9 | convolution fusion | flops 1080295424 | bytes 8652800 | tf_op jit(solution)/shard_map/dot_general | solution.py:37
  136.7 0.0 copy-done
  136.7 3.9 %convolution_convert_fusion = bf16[8192,256]{1,0:T(8,128)(2,1)} fusion(bf16[256,256]{1,0:T(8,128)(2,1)S(1)} %fusion.16, bf16[1,256,8192]{2,1,0:T(8,128)(2,1)S(1)} %copy-done, f32[256]{0:T(256)S(1)} %add_rsqrt_fusion), kind=kOutput, calls=%fused_computation.2 | convolution fusion | flops 1082130432 | bytes 8520704 | tf_op jit(solution)/shard_map/dot_general | solution.py:45
  140.6 0.0 copy-start.4
  140.6 0.0 copy-start.5
  140.6 0.0 reduce-scatter.2.cloned.1.call-update
  140.7 0.0 all-reduce.2.cloned.1.call-start
  140.7 0.5 all-reduce.2.cloned.1.call-update
  141.3 0.0 copy-done.6
  141.3 0.1 dynamic-slice_compare_fusion
  141.4 0.1 copy.15
  141.5 0.1 broadcast_bitcast_fusion
  141.6 0.3 copy.17
  141.9 70.4 %reduce-scatter.2.cloned.1.call-done = bf16[512,256]{1,0:T(8,128)(2,1)} async-done(((bf16[8192,256]{1,0:T(8,128)(2,1)}), bf16[512,256]{1,0:T(8,128)(2,1)}) %reduce-scatter.2.cloned.1.call-update) | async-done | bytes 262160 | tf_op jit(solution)/shard_map/reduce_scatter | solution.py:44
  212.2 1.7 fusion.23
  213.9 55.7 %all-reduce.2.cloned.1.call-done = bf16[512,256]{1,0:T(8,128)(2,1)} async-done(((bf16[512,256]{1,0:T(8,128)(2,1)}), bf16[512,256]{1,0:T(8,128)(2,1)}) %all-reduce.2.cloned.1.call-update) | async-done | bytes 262160 | tf_op jit(solution)/shard_map/psum | solution.py:60
  269.6 0.0 copy-done.1
  269.6 1.8 fusion.29
  271.4 74.5 %psum.14 = f32[]{:T(128)} all-reduce(f32[]{:T(128)} %fusion.23), channel_id=1, replica_groups=mesh['worker'=16,'fsdp'=16,'tensor'=2] {'fsdp','tensor'}, use_global_device_ids=true, to_apply=%region_3.0 | all-reduce | flops 1 | bytes 8 | tf_op jit(solution)/shard_map/psum | solution.py:52
  346.7 0.0 copy-done.2
  346.7 2.8 fusion.34
  (11 shorter events, 0.1 us)
Async XLA Ops:
  8.0 123.8 %copy-start.7 = (bf16[1,256,256]{2,1,0:T(8,128)(2,1)S(1)}, bf16[1,256,256]{2,1,0:T(8,128)(2,1)}, u32[]{:S(2)}) copy-start(bf16[1,256,256]{2,1,0:T(8,128)(2,1)} %param.12) | copy-start | bytes 393220
  8.0 76.7 %all-gather.5.cloned.1.call-start = ((), (), s32[]{:S(2)}) async-start(), calls=%async_computation.3 | async-start | bytes 6291456 | tf_op jit(solution)/shard_map/all_gather | solution.py:31
  8.7 123.1 %all-gather.7.cloned.1.call-start = ((), (), s32[]{:S(2)}) async-start(), calls=%async_computation.4 | async-start | bytes 4456448 | tf_op jit(solution)/shard_map/all_gather | solution.py:39
  9.5 202.8 %reduce-scatter.2.cloned.1.call-start = ((), (), s32[]{:S(2)}) async-start(), calls=%async_computation.1 | async-start | bytes 4456448 | tf_op jit(solution)/shard_map/reduce_scatter | solution.py:44
  131.8 4.9 %copy-start = (bf16[1,256,8192]{2,1,0:T(8,128)(2,1)S(1)}, bf16[1,256,8192]{2,1,0:T(8,128)(2,1)}, u32[]{:S(2)}) copy-start(bf16[1,256,8192]{2,1,0:T(8,128)(2,1)} %all-gather.5.cloned.1.call-done) | copy-start | bytes 12582916
  140.6 0.7 copy-start.6
  140.6 129.0 %copy-start.1 = (bf16[512,256]{1,0:T(8,128)(2,1)S(1)}, bf16[512,256]{1,0:T(8,128)(2,1)}, u32[]{:S(2)}) copy-start(bf16[512,256]{1,0:T(8,128)(2,1)} %param.18) | copy-start | bytes 786436
  140.6 206.1 %copy-start.2 = (bf16[1,512,256]{2,1,0:T(8,128)(2,1)S(1)}, bf16[1,512,256]{2,1,0:T(8,128)(2,1)}, u32[]{:S(2)}) copy-start(bf16[1,512,256]{2,1,0:T(8,128)(2,1)} %param.13) | copy-start | bytes 786436
  140.6 206.1 %copy-start.3 = (bf16[1,512,256]{2,1,0:T(8,128)(2,1)S(1)}, bf16[1,512,256]{2,1,0:T(8,128)(2,1)}, u32[]{:S(2)}) copy-start(bf16[1,512,256]{2,1,0:T(8,128)(2,1)} %param.15) | copy-start | bytes 786436
  140.6 206.1 %copy-start.4 = (bf16[1,512,256]{2,1,0:T(8,128)(2,1)S(1)}, bf16[1,512,256]{2,1,0:T(8,128)(2,1)}, u32[]{:S(2)}) copy-start(bf16[1,512,256]{2,1,0:T(8,128)(2,1)} %param.14) | copy-start | bytes 786436
  140.6 206.1 %copy-start.5 = (bf16[512,256]{1,0:T(8,128)(2,1)S(1)}, bf16[512,256]{1,0:T(8,128)(2,1)}, u32[]{:S(2)}) copy-start(bf16[512,256]{1,0:T(8,128)(2,1)} %param.17) | copy-start | bytes 786436
  140.7 128.9 %all-reduce.2.cloned.1.call-start = ((), (), s32[]{:S(2)}) async-start(), calls=%async_computation.2 | async-start | bytes 524288 | tf_op jit(solution)/shard_map/psum | solution.py:60
Sparse Core Ops, SparseCore 0:
  10.9 73.7 all-gather.4
  86.9 44.8 all-gather.6
  140.8 71.4 reduce-scatter.1
Sparse Core Ops, SparseCore 1:
  143.4 126.1 all-reduce.1
where the time goes:
time: 357 us
  waiting for transfers between devices  246 us (69%)
  blocking collectives  74.5 us (21%)
  between operations  16 us (4%)
  other arithmetic  10.1 us (3%)
  matrix products  8.78 us (2%)
    all_gather x1, waiting for transfers between devices, local(): whole = lax.all_gather(features_in[0], 'tensor', axis=1, tiled=True)  74.5 us
    psum x1, blocking collectives, local(): norm = jnp.sqrt(lax.psum(jnp.sum(raw * raw), ('fsdp', 'tensor')))  74.5 us
    reduce_scatter x1, waiting for transfers between devices, local(): lax.psum_scatter(lax.dot_general(columns, resid, (((0,), (0,)), ((), ()))...  70.4 us
    psum x1, waiting for transfers between devices, local(): lax.psum(delta.astype(jnp.bfloat16), 'worker').astype(jnp.float32)  55.7 us
    all_gather x1, waiting for transfers between devices, local(): lax.all_gather(weight, 'fsdp', axis=0, tiled=True)  43.9 us
  transfers between devices with their start and end apart: 4, of which 4 were waited for; matrix products, arithmetic and copies ran while one was open for 2% of the time, Pallas kernels for 0%

commit v1 on v0

v1 whole, which is shorter than its diff:
```python
import jax
import jax.numpy as jnp
from jax import lax
from jax.sharding import Mesh, PartitionSpec as P

HD = 128
WORKER = ("zh", "zl")
FSDP = ("ylo", "x", "core")
GROUP = ("x", "ylo")
PLANE = ("ylo", "x", "core", "tensor")
SIZES = {"ylo": 2, "x": 4, "core": 2, "tensor": 2}
BF = jnp.bfloat16
F32 = jnp.float32


def permute(value, axes, move):
    places = [()]
    for axis in axes:
        places = [p + (i,) for p in places for i in range(SIZES[axis])]
    number = {p: n for n, p in enumerate(places)}
    pairs = [(n, number[move(*p)]) for p, n in number.items()]
    return lax.ppermute(value, axes if len(axes) > 1 else axes[0], pairs)


def swap(value, axis):
    return permute(value, (axis,), lambda i: (1 - i,))


def local(
    token_ids,
    features_in,
    targets,
    local_weight,
    adam_first,
    adam_second,
    prev_delta,
    global_weight,
    outer_momentum,
    fragment_of_tile,
):
    weight = local_weight[0]
    rows, cols = weight.shape
    core = lax.axis_index("core")
    side = lax.axis_index("tensor")
    replicas = lax.axis_size("zh") * lax.axis_size("zl")
    group = lax.axis_size("x") * lax.axis_size("ylo")

    with jax.named_scope("outer_sum"):
        delta_sum = lax.psum(prev_delta[0], "zl")
        delta_sum = lax.psum(delta_sum, "zh").astype(F32)

    with jax.named_scope("weight_move"):
        moved = permute(weight, PLANE, lambda yl, x, c, t: (c, x, t, yl))

    with jax.named_scope("own_tokens"):
        mine = features_in[0]
        tokens, half = mine.shape
        squares = jnp.sum(jnp.square(mine.astype(F32)), axis=1)
        mask = (token_ids[0] != 0).astype(F32)
    with jax.named_scope("core_swap"):
        other = swap(mine, "core")
        note = jnp.concatenate(
            [targets[0].astype(F32), squares[None], mask[None]], axis=0
        )
        note_other = swap(note, "core")
    both = jnp.concatenate([mine, other], axis=0)
    target2 = jnp.concatenate([note[:tokens], note_other[:tokens]], axis=0)
    squares2 = jnp.concatenate([note[tokens], note_other[tokens]])
    mask2 = jnp.concatenate([note[tokens + 1], note_other[tokens + 1]])
    with jax.named_scope("squares_swap"):
        squares2 = squares2 + swap(squares2, "tensor")
    inv = lax.rsqrt(squares2 / (2 * half) + 1e-05)

    with jax.named_scope("weight_gather"):
        copies = jnp.broadcast_to(moved[None], (group, rows, cols))
        matrix = lax.all_to_all(copies, GROUP, 0, 0).reshape(group * rows, cols)

    with jax.named_scope("keys"):
        part = jnp.dot(both, matrix, preferred_element_type=F32) * inv[:, None]
        part = jnp.where(core == side, part - target2, part)
        theirs = swap(part.astype(BF), "tensor")
        scale = (inv * mask2)[:, None]
        resid = ((part + theirs.astype(F32)) * scale).astype(BF)

    with jax.named_scope("gradient"):
        term = lax.dot_general(
            both, resid, (((0,), (0,)), ((), ())), preferred_element_type=F32
        ).astype(BF)
        terms = lax.all_to_all(term.reshape(group, rows, cols), GROUP, 0, 0)
        total = jnp.sum(terms.astype(F32), axis=0)
    with jax.named_scope("gradient_home"):
        raw = permute(total.astype(BF), PLANE, lambda yl, x, c, t: (t, x, yl, c)).astype(F32)
    with jax.named_scope("norm"):
        partial = jnp.broadcast_to(jnp.sum(total * total), (32, 128))
        norm = jnp.sqrt(jnp.sum(lax.all_to_all(partial, PLANE, 0, 0)[:, 0]))

    clipped = raw * jnp.minimum(1.0, 1.0 / (norm + 1e-06))
    first = 0.9 * adam_first[0].astype(F32) + 0.1 * clipped
    second = 0.95 * adam_second[0].astype(F32) + 0.05 * clipped * clipped
    old = weight.astype(F32)
    stepped = old - 0.0004 * (first / (jnp.sqrt(second) + 1e-08) + 0.1 * old)

    outer_grad = delta_sum / replicas
    momentum = 0.9 * outer_momentum.astype(F32) + outer_grad
    merged = global_weight.astype(F32) - 0.7 * (outer_grad + 0.9 * momentum)
    heads = cols // HD
    tiles = lax.dynamic_slice_in_dim(fragment_of_tile, side * heads, heads, 1)
    selected = jnp.repeat(jnp.repeat(tiles == 0, HD, axis=0), HD, axis=1)
    new_momentum = jnp.where(selected, momentum.astype(BF), outer_momentum)
    new_global = jnp.where(selected, merged.astype(BF), global_weight)
    mixed = 0.5 * stepped + 0.5 * new_global.astype(F32)
    new_local = jnp.where(selected, mixed, stepped).astype(BF)
    return (
        new_local[None],
        first.astype(BF)[None],
        second.astype(BF)[None],
        new_global,
        new_momentum,
    )


def solution(mesh):
    fine = Mesh(
        mesh.devices.reshape(4, 4, *SIZES.values()), (*WORKER, *SIZES)
    )
    state = P(WORKER, FSDP, "tensor")
    outer = P(FSDP, "tensor")
    return jax.shard_map(
        local,
        mesh=fine,
        in_specs=(
            P(WORKER, FSDP),
            state,
            state,
            state,
            state,
            state,
            state,
            outer,
            outer,
            P(FSDP, None),
        ),
        out_specs=(state, state, state, outer, outer),
        check_vma=False,
    )
```

time: 357 us -> 230 us (0.64)
  waiting for transfers between devices: 246 us -> 153 us
  blocking collectives: 74.5 us -> 0 us
  starting transfers between devices: 0.16 us -> 42.8 us
    all_gather x2 -> x0, waiting for transfers between devices: 118 us -> none  [the longest x1 74.5 us: local(): whole = lax.all_gather(features_in[0], 'tensor', axis=1, tiled=True)]
    psum x1 -> x0, blocking collectives: 74.5 us -> none  [local(): norm = jnp.sqrt(lax.psum(jnp.sum(raw * raw), ('fsdp', 'tensor')))]
    reduce_scatter x1 -> x0, waiting for transfers between devices: 70.4 us -> none  [local(): lax.psum_scatter(lax.dot_general(columns, resid, (((0,), (0,)), ((), ()))...]
    psum x1 -> x2, waiting for transfers between devices: 55.7 us -> 120 us  [the longest x1 64.1 us: local(): delta_sum = lax.psum(prev_delta[0], 'zl')]
    ppermute x0 -> x6, starting transfers between devices: none -> 24.8 us  [permute(): return lax.ppermute(value, axes if len(axes) > 1 else axes[0], pairs)]
    ppermute x0 -> x6, waiting for transfers between devices: none -> 19.3 us  [permute(): return lax.ppermute(value, axes if len(axes) > 1 else axes[0], pairs)]
    all_to_all x0 -> x3, starting transfers between devices: none -> 17.9 us  [the longest x1 9.66 us: local(): norm = jnp.sqrt(jnp.sum(lax.all_to_all(partial, PLANE, 0, 0)[:, 0]))]
    all_to_all x0 -> x3, waiting for transfers between devices: none -> 12.8 us  [the longest x1 12.8 us: local(): matrix = lax.all_to_all(copies, GROUP, 0, 0).reshape(group * rows, cols)]
  transfers between devices with their start and end apart: 4 -> 11, of which waited for: 4 -> 7; matrix products, arithmetic and copies ran while one was open for 2% -> 3% of each run, Pallas kernels for 0% -> 0%
where the time goes in v1:
time: 230 us; the launch traced here: 229 us
  waiting for transfers between devices  153 us (67%)
  starting transfers between devices  42.8 us (19%)
  between operations  15 us (7%)
  matrix products  7.79 us (3%)
  other arithmetic  6.76 us (3%)
  local copies, waits for them, and re-layouts  3.3 us (1%)
    psum x1, waiting for transfers between devices, local(): delta_sum = lax.psum(prev_delta[0], 'zl')  64.1 us
    psum x1, waiting for transfers between devices, local(): delta_sum = lax.psum(delta_sum, 'zh').astype(F32)  56.4 us
    ppermute x6, starting transfers between devices, permute(): return lax.ppermute(value, axes if len(axes) > 1 else axes[0], pairs)  24.8 us
    ppermute x6, waiting for transfers between devices, permute(): return lax.ppermute(value, axes if len(axes) > 1 else axes[0], pairs)  19.3 us
    all_to_all x1, waiting for transfers between devices, local(): matrix = lax.all_to_all(copies, GROUP, 0, 0).reshape(group * rows, cols)  12.8 us
    all_to_all x1, starting transfers between devices, local(): norm = jnp.sqrt(jnp.sum(lax.all_to_all(partial, PLANE, 0, 0)[:, 0]))  9.66 us
  transfers between devices with their start and end apart: 11, of which 7 were waited for; matrix products, arithmetic and copies ran while one was open for 3% of the time, Pallas kernels for 0%

profile of v1, /device:TPU:1, one launch (start us, length us, event | category | flops | bytes accessed | tf_op | source)
XLA Modules:
  0.0 228.9 jit_solution(6014934349597191243)
XLA Ops:
  7.2 4.6 %collective-permute-start.1 = (bf16[512,256]{1,0:T(8,128)(2,1)}, bf16[512,256]{1,0:T(8,128)(2,1)S(1)}, u32[]{:S(2)}, u32[]{:S(2)}) collective-permute-start(bf16[512,256]{1,0:T(8,128)(2,1)} %bitcast.55), channel_id=1, source_target_pairs={{0,0},{1,2},{2,16},{3,18},{4,4},{5,6},{6,20},{7,22},{8,8},{9,10},{... | collective-permute-start | bytes 786440 | tf_op jit(solution)/shard_map/weight_move/ppermute | solution.py:22
  11.8 5.8 %collective-permute-start = (bf16[256,4096]{1,0:T(8,128)(2,1)}, bf16[256,4096]{1,0:T(8,128)(2,1)}, u32[]{:S(2)}, u32[]{:S(2)}) collective-permute-start(bf16[256,4096]{1,0:T(8,128)(2,1)} %bitcast.50), channel_id=1, source_target_pairs={{0,2},{2,0},{1,3},{3,1},{4,6},{6,4},{5,7},{7,5},{8,10},{10,8},{9,1... | collective-permute-start | bytes 6291464 | tf_op jit(solution)/shard_map/core_swap/ppermute | solution.py:22
  17.6 0.1 collective-permute-done.1
  17.6 1.5 broadcast_in_dim.32
  19.1 4.5 %all-to-all-start = ((bf16[8,512,256]{2,1,0:T(8,128)(2,1)}), bf16[8,512,256]{2,1,0:T(8,128)(2,1)}, u32[]{:S(2)}, u32[]{:S(2)}) async-start(bf16[8,512,256]{2,1,0:T(8,128)(2,1)} %broadcast_in_dim.32), calls=%async_computation | async-start | bytes 4194304 | tf_op jit(solution)/shard_map/weight_gather/all_to_all | solution.py:76
  23.7 0.5 multiply_reduce_fusion
  24.2 1.9 collective-permute-start.2
  26.1 1.5 collective-permute-done.2
  27.7 5.5 %collective-permute-start.3 = (f32[512]{0:T(512)S(1)}, f32[512]{0:T(512)S(1)}, u32[]{:S(2)}, u32[]{:S(2)}) collective-permute-start(f32[512]{0:T(512)S(1)} %pad_maximum_fusion.8), channel_id=1, source_target_pairs={{0,1},{1,0},{2,3},{3,2},{4,5},{5,4},{6,7},{7,6},{8,9},{9,8},{10,11... | collective-permute-start | bytes 6152 | tf_op jit(solution)/shard_map/squares_swap/ppermute | solution.py:22
  33.2 9.2 %collective-permute-done.3 = f32[512]{0:T(512)S(1)} collective-permute-done((f32[512]{0:T(512)S(1)}, f32[512]{0:T(512)S(1)}, u32[]{:S(2)}, u32[]{:S(2)}) %collective-permute-start.3) | collective-permute-done | bytes 2080 | tf_op jit(solution)/shard_map/squares_swap/ppermute | solution.py:22
  42.4 12.8 %all-to-all-done = bf16[8,512,256]{2,1,0:T(8,128)(2,1)} async-done(((bf16[8,512,256]{2,1,0:T(8,128)(2,1)}), bf16[8,512,256]{2,1,0:T(8,128)(2,1)}, u32[]{:S(2)}, u32[]{:S(2)}) %all-to-all-start) | async-done | bytes 2097184 | tf_op jit(solution)/shard_map/weight_gather/all_to_all | solution.py:76
  55.2 3.5 %fusion.19 = (bf16[512,256]{1,0:T(8,128)(2,1)S(1)}, f32[512,256]{1,0:T(8,128)S(1)}) fusion(f32[256,256]{1,0:T(8,128)S(1)} %slice.17, f32[256,256]{1,0:T(8,128)S(1)} %bitcast_convert_fusion, f32[512]{0:T(512)S(1)} %get-tuple-element.13, bf16[4096,256]{1,0:T(8,128)(2,1)} %bitcast.4, bf16[256,4096]{1,0:T(8,128)(2,1)} %collective-permute-done, ...), kind=kOutput, calls=%fused_computation.44 | convolution fusion | flops 1082785792 | bytes 7604225 | tf_op jit(solution)/shard_map/keys/dot_general | solution.py:79
  58.7 1.9 collective-permute-start.4
  60.7 8.5 %collective-permute-done.4 = bf16[512,256]{1,0:T(8,128)(2,1)S(1)} collective-permute-done((bf16[512,256]{1,0:T(8,128)(2,1)S(1)}, bf16[512,256]{1,0:T(8,128)(2,1)S(1)}, u32[]{:S(2)}, u32[]{:S(2)}) %collective-permute-start.4) | collective-permute-done | bytes 262176 | tf_op jit(solution)/shard_map/keys/ppermute | solution.py:22
  69.2 4.3 %convolution_convert_fusion = bf16[4096,256]{1,0:T(8,128)(2,1)} fusion(bf16[256,4096]{1,0:T(8,128)(2,1)} %collective-permute-done, bf16[256,4096]{1,0:T(8,128)(2,1)S(1)} %bitcast.52, f32[512,256]{1,0:T(8,128)S(1)} %get-tuple-element.21, bf16[512,256]{1,0:T(8,128)(2,1)S(1)} %collective-permute-done.4, f32[512]{0:T(512)S(1)} %get-tuple-element.12), kind=kOutput, calls=%fused_computation | convolution fusion | flops 1083703296 | bytes 7079936 | tf_op jit(solution)/shard_map/gradient/dot_general | solution.py:86
  73.5 3.7 %all-to-all-start.1 = ((bf16[8,512,256]{2,1,0:T(8,128)(2,1)}), bf16[8,512,256]{2,1,0:T(8,128)(2,1)S(1)}, u32[]{:S(2)}, u32[]{:S(2)}) async-start(bf16[8,512,256]{2,1,0:T(8,128)(2,1)} %bitcast.53), calls=%async_computation.1 | async-start | bytes 4194304 | tf_op jit(solution)/shard_map/gradient/all_to_all | solution.py:89
  77.2 0.0 all-reduce.3.cloned.1.call-start
  77.3 0.7 all-reduce.3.cloned.1.call-update
  78.0 0.1 dynamic-slice_compare_fusion
  78.1 0.1 copy.38
  78.2 0.1 broadcast_bitcast_fusion
  78.4 0.3 copy.41
  78.6 64.1 %all-reduce.3.cloned.1.call-done = bf16[512,256]{1,0:T(8,128)(2,1)} async-done(((bf16[512,256]{1,0:T(8,128)(2,1)}), bf16[512,256]{1,0:T(8,128)(2,1)}) %all-reduce.3.cloned.1.call-update) | async-done | bytes 262160 | tf_op jit(solution)/shard_map/outer_sum/psum | solution.py:49
  142.8 0.3 convert_reduce_fusion
  143.1 0.7 fusion.17
  143.8 1.3 broadcast_in_dim.34
  145.1 9.7 %all-to-all-start.2 = ((f32[32,1,128]{2,1,0:T(1,128)}), f32[32,1,128]{2,1,0:T(1,128)S(1)}, u32[]{:S(2)}, u32[]{:S(2)}) async-start(f32[32,1,128]{2,1,0:T(1,128)} %broadcast_in_dim.34), calls=%async_computation.2 | async-start | bytes 32768 | tf_op jit(solution)/shard_map/norm/all_to_all | solution.py:95
  154.8 5.0 %collective-permute-start.5 = (bf16[512,256]{1,0:T(8,128)(2,1)S(1)}, bf16[512,256]{1,0:T(8,128)(2,1)S(1)}, u32[]{:S(2)}, u32[]{:S(2)}) collective-permute-start(bf16[512,256]{1,0:T(8,128)(2,1)S(1)} %get-tuple-element.16), channel_id=1, source_target_pairs={{0,0},{1,16},{2,1},{3,17},{4,4},{5,20},{6,5},{7,21},{8,8},{9,24},{... | collective-permute-start | bytes 786440 | tf_op jit(solution)/shard_map/gradient_home/ppermute | solution.py:22
  159.8 56.4 %all-reduce.5.cloned.1.call-done = bf16[512,256]{1,0:T(8,128)(2,1)} async-done(((bf16[512,256]{1,0:T(8,128)(2,1)}), bf16[512,256]{1,0:T(8,128)(2,1)}) %all-reduce.5.cloned.1.call-update) | async-done | bytes 262160 | tf_op jit(solution)/shard_map/outer_sum/psum | solution.py:50
  216.2 1.8 fusion.7
  218.0 0.6 slice_reduce_fusion
  219.4 2.7 %fusion.13 = (bf16[1,512,256]{2,1,0:T(8,128)(2,1)}, bf16[512,256]{1,0:T(8,128)(2,1)}, bf16[1,512,256]{2,1,0:T(8,128)(2,1)}, bf16[1,512,256]{2,1,0:T(8,128)(2,1)}) fusion(pred[512,256]{1,0:T(8,128)(4,1)S(1)} %copy.41, bf16[1,512,256]{2,1,0:T(8,128)(2,1)S(1)} %copy-done.2, f32[]{:T(128)S(6)} %min.3, bf16[512,256]{1,0:T(8,128)(2,1)S(1)} %collective-permute-done.5, ...), kind=kLoop, calls=%fused_computation.30 | loop fusion | flops 4849664 | bytes 3014660 | tf_op jit(solution)/shard_map/broadcast_in_dim | solution.py:114
  (33 shorter events, 0.3 us)
Async XLA Ops:
  7.2 10.5 %collective-permute-start.1 = (bf16[512,256]{1,0:T(8,128)(2,1)}, bf16[512,256]{1,0:T(8,128)(2,1)S(1)}, u32[]{:S(2)}, u32[]{:S(2)}) collective-permute-start(bf16[512,256]{1,0:T(8,128)(2,1)} %bitcast.55), channel_id=1, source_target_pairs={{0,0},{1,2},{2,16},{3,18},{4,4},{5,6},{6,20},{7,22},{8,8},{9,10},{... | collective-permute-start | bytes 786440 | tf_op jit(solution)/shard_map/weight_move/ppermute | solution.py:22
  11.8 43.5 %collective-permute-start = (bf16[256,4096]{1,0:T(8,128)(2,1)}, bf16[256,4096]{1,0:T(8,128)(2,1)}, u32[]{:S(2)}, u32[]{:S(2)}) collective-permute-start(bf16[256,4096]{1,0:T(8,128)(2,1)} %bitcast.50), channel_id=1, source_target_pairs={{0,2},{2,0},{1,3},{3,1},{4,6},{6,4},{5,7},{7,5},{8,10},{10,8},{9,1... | collective-permute-start | bytes 6291464 | tf_op jit(solution)/shard_map/core_swap/ppermute | solution.py:22
  19.1 4.5 %copy-start.8 = (s32[1,256]{1,0:T(1,128)S(1)}, s32[1,256]{1,0:T(1,128)}, u32[]{:S(2)}) copy-start(s32[1,256]{1,0:T(1,128)} %param.10) | copy-start | bytes 3076
  19.1 4.5 %copy-start.6 = (bf16[1,256,256]{2,1,0:T(8,128)(2,1)S(1)}, bf16[1,256,256]{2,1,0:T(8,128)(2,1)}, u32[]{:S(2)}) copy-start(bf16[1,256,256]{2,1,0:T(8,128)(2,1)} %param.12) | copy-start | bytes 393220
  19.1 4.6 %copy-start = (bf16[1,256,4096]{2,1,0:T(8,128)(2,1)S(1)}, bf16[1,256,4096]{2,1,0:T(8,128)(2,1)}, u32[]{:S(2)}) copy-start(bf16[1,256,4096]{2,1,0:T(8,128)(2,1)} %param.11) | copy-start | bytes 6291460
  19.1 36.1 %all-to-all-start = ((bf16[8,512,256]{2,1,0:T(8,128)(2,1)}), bf16[8,512,256]{2,1,0:T(8,128)(2,1)}, u32[]{:S(2)}, u32[]{:S(2)}) async-start(bf16[8,512,256]{2,1,0:T(8,128)(2,1)} %broadcast_in_dim.32), calls=%async_computation | async-start | bytes 4194304 | tf_op jit(solution)/shard_map/weight_gather/all_to_all | solution.py:76
  24.2 3.4 %collective-permute-start.2 = (f32[258,256]{1,0:T(8,128)S(1)}, f32[258,256]{1,0:T(8,128)S(1)}, u32[]{:S(2)}, u32[]{:S(2)}) collective-permute-start(f32[258,256]{1,0:T(8,128)S(1)} %pad_maximum_fusion.7), channel_id=1, source_target_pairs={{0,2},{2,0},{1,3},{3,1},{4,6},{6,4},{5,7},{7,5},{8,10},{10,8},{9,1... | collective-permute-start | bytes 792584 | tf_op jit(solution)/shard_map/core_swap/ppermute | solution.py:22
  27.7 14.7 %collective-permute-start.3 = (f32[512]{0:T(512)S(1)}, f32[512]{0:T(512)S(1)}, u32[]{:S(2)}, u32[]{:S(2)}) collective-permute-start(f32[512]{0:T(512)S(1)} %pad_maximum_fusion.8), channel_id=1, source_target_pairs={{0,1},{1,0},{2,3},{3,2},{4,5},{5,4},{6,7},{7,6},{8,9},{9,8},{10,11... | collective-permute-start | bytes 6152 | tf_op jit(solution)/shard_map/squares_swap/ppermute | solution.py:22
  58.7 10.5 %collective-permute-start.4 = (bf16[512,256]{1,0:T(8,128)(2,1)S(1)}, bf16[512,256]{1,0:T(8,128)(2,1)S(1)}, u32[]{:S(2)}, u32[]{:S(2)}) collective-permute-start(bf16[512,256]{1,0:T(8,128)(2,1)S(1)} %get-tuple-element.20), channel_id=1, source_target_pairs={{0,1},{1,0},{2,3},{3,2},{4,5},{5,4},{6,7},{7,6},{8,9},{9,8},{10,11... | collective-permute-start | bytes 786440 | tf_op jit(solution)/shard_map/keys/ppermute | solution.py:22
  73.5 4.5 %copy-start.7 = (s32[4,4]{1,0:T(4,128)S(1)}, s32[4,4]{1,0:T(4,128)}, u32[]{:S(2)}) copy-start(s32[4,4]{1,0:T(4,128)} %param.19) | copy-start | bytes 196
  73.5 69.3 %all-to-all-start.1 = ((bf16[8,512,256]{2,1,0:T(8,128)(2,1)}), bf16[8,512,256]{2,1,0:T(8,128)(2,1)S(1)}, u32[]{:S(2)}, u32[]{:S(2)}) async-start(bf16[8,512,256]{2,1,0:T(8,128)(2,1)} %bitcast.53), calls=%async_computation.1 | async-start | bytes 4194304 | tf_op jit(solution)/shard_map/gradient/all_to_all | solution.py:89
  77.2 65.5 %all-reduce.3.cloned.1.call-start = ((), (), s32[]{:S(2)}) async-start(), calls=%async_computation.3 | async-start | bytes 524288 | tf_op jit(solution)/shard_map/outer_sum/psum | solution.py:49
  78.0 138.2 %copy-start.1 = (bf16[512,256]{1,0:T(8,128)(2,1)S(1)}, bf16[512,256]{1,0:T(8,128)(2,1)}, u32[]{:S(2)}) copy-start(bf16[512,256]{1,0:T(8,128)(2,1)} %param.18) | copy-start | bytes 786436
  78.0 138.2 %all-reduce.5.cloned.1.call-start = ((), (), s32[]{:S(2)}) async-start(), calls=%async_computation.4 | async-start | bytes 524288 | tf_op jit(solution)/shard_map/outer_sum/psum | solution.py:50
  142.8 76.6 %copy-start.2 = (bf16[1,512,256]{2,1,0:T(8,128)(2,1)S(1)}, bf16[1,512,256]{2,1,0:T(8,128)(2,1)}, u32[]{:S(2)}) copy-start(bf16[1,512,256]{2,1,0:T(8,128)(2,1)} %param.15) | copy-start | bytes 786436
  142.8 76.6 %copy-start.3 = (bf16[1,512,256]{2,1,0:T(8,128)(2,1)S(1)}, bf16[1,512,256]{2,1,0:T(8,128)(2,1)}, u32[]{:S(2)}) copy-start(bf16[1,512,256]{2,1,0:T(8,128)(2,1)} %param.13) | copy-start | bytes 786436
  142.8 76.6 %copy-start.4 = (bf16[1,512,256]{2,1,0:T(8,128)(2,1)S(1)}, bf16[1,512,256]{2,1,0:T(8,128)(2,1)}, u32[]{:S(2)}) copy-start(bf16[1,512,256]{2,1,0:T(8,128)(2,1)} %param.14) | copy-start | bytes 786436
  142.8 76.6 %copy-start.5 = (bf16[512,256]{1,0:T(8,128)(2,1)S(1)}, bf16[512,256]{1,0:T(8,128)(2,1)}, u32[]{:S(2)}) copy-start(bf16[512,256]{1,0:T(8,128)(2,1)} %param.17) | copy-start | bytes 786436
  145.1 72.9 %all-to-all-start.2 = ((f32[32,1,128]{2,1,0:T(1,128)}), f32[32,1,128]{2,1,0:T(1,128)S(1)}, u32[]{:S(2)}, u32[]{:S(2)}) async-start(f32[32,1,128]{2,1,0:T(1,128)} %broadcast_in_dim.34), calls=%async_computation.2 | async-start | bytes 32768 | tf_op jit(solution)/shard_map/norm/all_to_all | solution.py:95
  154.8 64.6 %collective-permute-start.5 = (bf16[512,256]{1,0:T(8,128)(2,1)S(1)}, bf16[512,256]{1,0:T(8,128)(2,1)S(1)}, u32[]{:S(2)}, u32[]{:S(2)}) collective-permute-start(bf16[512,256]{1,0:T(8,128)(2,1)S(1)} %get-tuple-element.16), channel_id=1, source_target_pairs={{0,0},{1,16},{2,1},{3,17},{4,4},{5,20},{6,5},{7,21},{8,8},{9,24},{... | collective-permute-start | bytes 786440 | tf_op jit(solution)/shard_map/gradient_home/ppermute | solution.py:22
Sparse Core Ops, SparseCore 0:
  81.0 61.6 all-reduce.2
  145.9 70.2 all-reduce.4

commit v2 on v1

v2 whole, which is shorter than its diff:
```python
import jax
import jax.numpy as jnp
from jax import lax
from jax.experimental import pallas as pl
from jax.experimental.pallas import tpu as pltpu
from jax.sharding import Mesh, PartitionSpec as P

HD = 128
WORKER = "worker"
FSDP = ("ylo", "x", "core")
GROUP = ("x", "ylo")
PLANE = ("ylo", "x", "core", "tensor")
SIZES = {
    "worker": 16,
    "ylo": 2,
    "x": 4,
    "core": 2,
    "tensor": 2,
}
BF = jnp.bfloat16
F32 = jnp.float32
VMEM_LIMIT = 32 * 2**20


def permute(value, axes, move):
    places = [()]
    for axis in axes:
        places = [p + (i,) for p in places for i in range(SIZES[axis])]
    number = {p: n for n, p in enumerate(places)}
    pairs = [(n, number[move(*p)]) for p, n in number.items()]
    return lax.ppermute(value, axes if len(axes) > 1 else axes[0], pairs)


def swap(value, axis):
    return permute(value, (axis,), lambda i: (1 - i,))


def after(value, *others):
    return lax.optimization_barrier((value, *others))[0]


def call(kernel, name, grid, ins, in_specs, outs, out_specs, scratch=(), flops=0):
    moved = sum(a.size * a.dtype.itemsize for a in (*ins, *outs))
    return pl.pallas_call(
        kernel,
        grid=grid,
        in_specs=in_specs,
        out_specs=out_specs,
        out_shape=outs,
        scratch_shapes=scratch,
        name=name,
        compiler_params=pltpu.CompilerParams(vmem_limit_bytes=VMEM_LIMIT),
        cost_estimate=pl.CostEstimate(
            flops=flops, bytes_accessed=moved, transcendentals=0
        ),
    )(*ins)


def sum_kernel(terms, total, squares, so_far):
    step = pl.program_id(0)
    value = jnp.sum(terms[...].astype(F32), axis=0)
    total[...] = value.astype(BF)

    @pl.when(step == 0)
    def _():
        so_far[...] = jnp.zeros_like(so_far)

    so_far[...] += jnp.sum(value * value, axis=0, keepdims=True)

    @pl.when(step == pl.num_programs(0) - 1)
    def _():
        squares[...] = jnp.full(squares.shape, jnp.sum(so_far[...]), F32)


def sum_terms(terms, places):
    group, rows, cols = terms.shape
    part = rows // 4
    return call(
        sum_kernel,
        "sum_terms",
        (rows // part,),
        (terms,),
        [pl.BlockSpec((group, part, cols), lambda k: (0, k, 0))],
        [
            jax.ShapeDtypeStruct((rows, cols), BF),
            jax.ShapeDtypeStruct((places, 128), F32),
        ],
        [
            pl.BlockSpec((part, cols), lambda k: (k, 0)),
            pl.BlockSpec((places, 128), lambda k: (0, 0)),
        ],
        [pltpu.VMEM((1, cols), F32)],
    )


def update_kernel(
    replicas,
    spot,
    fragment,
    squares,
    raw,
    adam_first,
    adam_second,
    weight,
    global_weight,
    outer_momentum,
    delta_sum,
    new_local,
    new_first,
    new_second,
    new_global,
    new_momentum,
):
    step = pl.program_id(0)
    norm = jnp.sqrt(jnp.sum(squares[...], axis=0, keepdims=True)[:, :1])
    clip = jnp.minimum(1.0, 1.0 / (norm + 1e-06))
    heads = raw.shape[1] // HD
    for head in range(heads):
        at = (slice(None), slice(head * HD, (head + 1) * HD))
        clipped = raw[at].astype(F32) * clip
        first = 0.9 * adam_first[at].astype(F32) + 0.1 * clipped
        second = 0.95 * adam_second[at].astype(F32) + 0.05 * clipped * clipped
        old = weight[at].astype(F32)
        stepped = old - 0.0004 * (first / (jnp.sqrt(second) + 1e-08) + 0.1 * old)
        new_first[at] = first.astype(BF)
        new_second[at] = second.astype(BF)
        chosen = fragment[step, spot[0] * heads + head] == 0

        @pl.when(chosen)
        def _():
            outer_grad = delta_sum[at] / replicas
            momentum = 0.9 * outer_momentum[at].astype(F32) + outer_grad
            merged = global_weight[at].astype(F32) - 0.7 * (
                outer_grad + 0.9 * momentum
            )
            merged = merged.astype(BF)
            new_momentum[at] = momentum.astype(BF)
            new_global[at] = merged
            new_local[at] = (0.5 * stepped + 0.5 * merged.astype(F32)).astype(BF)

        @pl.when(jnp.logical_not(chosen))
        def _():
            new_momentum[at] = outer_momentum[at]
            new_global[at] = global_weight[at]
            new_local[at] = stepped.astype(BF)


def update(replicas, spot, fragment, squares, arrays):
    rows, cols = arrays[0].shape
    block = pl.BlockSpec((HD, cols), lambda k: (k, 0))
    smem = pl.BlockSpec(memory_space=pltpu.SMEM)
    return call(
        lambda *refs: update_kernel(replicas, *refs),
        "update",
        (rows // HD,),
        (spot, fragment, squares, *arrays),
        [smem, smem, pl.BlockSpec(squares.shape, lambda k: (0, 0))]
        + [block] * len(arrays),
        [jax.ShapeDtypeStruct((rows, cols), BF)] * 5,
        [block] * 5,
    )


def local(
    token_ids,
    features_in,
    targets,
    local_weight,
    adam_first,
    adam_second,
    prev_delta,
    global_weight,
    outer_momentum,
    fragment_of_tile,
):
    weight = local_weight[0]
    rows, cols = weight.shape
    core = lax.axis_index("core")
    side = lax.axis_index("tensor")
    replicas = lax.axis_size(WORKER)
    group = lax.axis_size("x") * lax.axis_size("ylo")
    mine = features_in[0]
    tokens, half = mine.shape

    with jax.named_scope("weight_move"):
        moved = permute(weight, PLANE, lambda yl, x, c, t: (c, x, t, yl))

    with jax.named_scope("squares"):
        squares = jnp.sum(jnp.square(mine.astype(F32)), axis=1)
        squares = squares + swap(squares, "tensor")

    with jax.named_scope("weight_gather"):
        copies = jnp.broadcast_to(moved[None], (group, rows, cols))
        copies, squares = lax.optimization_barrier((copies, squares))
        matrix = lax.all_to_all(copies, GROUP, 0, 0).reshape(group * rows, cols)

    with jax.named_scope("core_swap"):
        inv = lax.rsqrt(squares / (2 * half) + 1e-05)
        mask = (token_ids[0] != 0).astype(F32)
        note = jnp.concatenate(
            [targets[0].astype(F32), inv[None], mask[None]], axis=0
        )
        note_other = swap(note, "core")
        other = swap(after(mine, copies), "core")
        both = jnp.concatenate([mine, other], axis=0)
        target2 = jnp.concatenate([note[:tokens], note_other[:tokens]], axis=0)
        inv2 = jnp.concatenate([note[tokens], note_other[tokens]])
        mask2 = jnp.concatenate([note[tokens + 1], note_other[tokens + 1]])

    with jax.named_scope("outer_gather"):
        deltas = lax.all_gather(prev_delta[0], WORKER)

    with jax.named_scope("keys"):
        part = jnp.dot(both, matrix, preferred_element_type=F32) * inv2[:, None]
        part = jnp.where(core == side, part - target2, part)
        theirs = swap(part.astype(BF), "tensor")
        scale = (inv2 * mask2)[:, None]
        resid = ((part + theirs.astype(F32)) * scale).astype(BF)

    with jax.named_scope("gradient"):
        term = lax.dot_general(
            both, resid, (((0,), (0,)), ((), ())), preferred_element_type=F32
        ).astype(BF)
        terms = lax.all_to_all(term.reshape(group, rows, cols), GROUP, 0, 0)
        terms, deltas = lax.optimization_barrier((terms, deltas))
        total, partial = sum_terms(terms, 32)
        delta_sum = jnp.sum(deltas.astype(F32), axis=0)

    with jax.named_scope("gradient_home"):
        raw = permute(total, PLANE, lambda yl, x, c, t: (t, x, yl, c))
    with jax.named_scope("norm"):
        partial = lax.all_to_all(partial, PLANE, 0, 0, tiled=True)

    outs = update(
        replicas,
        side.reshape(1),
        fragment_of_tile,
        partial,
        [
            raw,
            adam_first[0],
            adam_second[0],
            weight,
            global_weight,
            outer_momentum,
            delta_sum,
        ],
    )
    return (outs[0][None], outs[1][None], outs[2][None], outs[3], outs[4])


def solution(mesh):
    fine = Mesh(mesh.devices.reshape(*SIZES.values()), tuple(SIZES))
    state = P(WORKER, FSDP, "tensor")
    outer = P(FSDP, "tensor")
    return jax.shard_map(
        local,
        mesh=fine,
        in_specs=(
            P(WORKER, FSDP),
            state,
            state,
            state,
            state,
            state,
            state,
            outer,
            outer,
            P(FSDP, None),
        ),
        out_specs=(state, state, state, outer, outer),
        check_vma=False,
    )
```

time: 230 us -> 138 us (0.60)
  waiting for transfers between devices: 153 us -> 45.4 us
  blocking collectives: 0 us -> 27 us
  starting transfers between devices: 42.8 us -> 33.2 us
  Pallas kernels: 0 us -> 4.74 us
    psum x2 -> x0, waiting for transfers between devices: 120 us -> none  [the longest x1 64.1 us: local(): delta_sum = lax.psum(prev_delta[0], 'zl')]
    all_to_all x0 -> x1, blocking collectives: none -> 27 us  [local(): terms = lax.all_to_all(term.reshape(group, rows, cols), GROUP, 0, 0)]
    all_to_all x1, waiting for transfers between devices: 12.8 us -> 28 us  [local(): matrix = lax.all_to_all(copies, GROUP, 0, 0).reshape(group * rows, cols)]
    all_to_all x2 -> x1, starting transfers between devices: 13.4 us -> 4.67 us  [local(): partial = lax.all_to_all(partial, PLANE, 0, 0, tiled=True)]
    ppermute x6, waiting for transfers between devices: 19.3 us -> 12.7 us  [permute(): return lax.ppermute(value, axes if len(axes) > 1 else axes[0], pairs)]
    pallas_call x0 -> x2, Pallas kernels: none -> 4.74 us  [call(): pl.pallas_call(kernel, grid=grid, in_specs=in_specs, out_specs=out_specs,...]
    all_to_all x2 -> x1, waiting for transfers between devices: 0.01 us -> 3.99 us  [local(): partial = lax.all_to_all(partial, PLANE, 0, 0, tiled=True)]
    broadcast_in_dim x1 -> x0, other arithmetic: 2.7 us -> none  [local(): new_local[None]]
  transfers between devices with their start and end apart: 11 -> 9, of which waited for: 7 -> 5; matrix products, arithmetic and copies ran while one was open for 3% -> 9% of each run, Pallas kernels for 0% -> 0%
where the time goes in v2:
time: 138 us
  waiting for transfers between devices  45.4 us (33%)
  starting transfers between devices  33.2 us (24%)
  blocking collectives  27 us (20%)
  between operations  14.3 us (10%)
  matrix products  6.51 us (5%)
  other arithmetic  4.97 us (4%)
  Pallas kernels  4.74 us (3%)
  local copies, waits for them, and re-layouts  1.57 us (1%)
    all_to_all x1, waiting for transfers between devices, local(): matrix = lax.all_to_all(copies, GROUP, 0, 0).reshape(group * rows, cols)  28 us
    all_to_all x1, blocking collectives, local(): terms = lax.all_to_all(term.reshape(group, rows, cols), GROUP, 0, 0)  27 us
    ppermute x6, starting transfers between devices, permute(): return lax.ppermute(value, axes if len(axes) > 1 else axes[0], pairs)  24.1 us
    ppermute x6, waiting for transfers between devices, permute(): return lax.ppermute(value, axes if len(axes) > 1 else axes[0], pairs)  12.7 us
    pallas_call x2, Pallas kernels, call(): pl.pallas_call(kernel, grid=grid, in_specs=in_specs, out_specs=out_specs,...  4.74 us
    all_to_all x1, starting transfers between devices, local(): partial = lax.all_to_all(partial, PLANE, 0, 0, tiled=True)  4.67 us
    all_to_all x1, starting transfers between devices, local(): matrix = lax.all_to_all(copies, GROUP, 0, 0).reshape(group * rows, cols)  4.36 us
    all_to_all x1, waiting for transfers between devices, local(): partial = lax.all_to_all(partial, PLANE, 0, 0, tiled=True)  3.99 us
  transfers between devices with their start and end apart: 9, of which 5 were waited for; matrix products, arithmetic and copies ran while one was open for 9% of the time, Pallas kernels for 0%

profile of v2, /device:TPU:1, one launch (start us, length us, event | category | flops | bytes accessed | tf_op | source)
XLA Modules:
  0.0 137.7 jit_solution(14987040737475805983)
XLA Ops:
  7.2 0.0 copy-start.6
  7.2 0.0 all-gather.2.cloned.1.call-start
  7.2 0.7 all-gather.2.cloned.1.call-update
  7.9 0.0 copy-start.8
  7.9 0.0 copy-start.7
  7.9 4.7 %collective-permute-start = (bf16[512,256]{1,0:T(8,128)(2,1)}, bf16[512,256]{1,0:T(8,128)(2,1)S(1)}, u32[]{:S(2)}, u32[]{:S(2)}) collective-permute-start(bf16[512,256]{1,0:T(8,128)(2,1)} %bitcast.23), channel_id=1, source_target_pairs={{0,0},{1,2},{2,16},{3,18},{4,4},{5,6},{6,20},{7,22},{8,8},{9,10},{... | collective-permute-start | bytes 786440 | tf_op jit(solution)/shard_map/weight_move/ppermute | solution.py:31
  12.7 2.1 %multiply_reduce_fusion = f32[256]{0:T(256)S(1)} fusion(bf16[1,256,4096]{2,1,0:T(8,128)(2,1)} %param.11), kind=kLoop, calls=%fused_computation.3 | loop fusion | flops 3145472 | bytes 2098176 | tf_op jit(solution)/shard_map/squares/reduce_sum | solution.py:189
  14.8 3.1 %collective-permute-start.1 = (f32[256]{0:T(256)S(1)}, f32[256]{0:T(256)S(1)}, u32[]{:S(2)}, u32[]{:S(2)}) collective-permute-start(f32[256]{0:T(256)S(1)} %multiply_reduce_fusion), channel_id=1, source_target_pairs={{0,1},{1,0},{2,3},{3,2},{4,5},{5,4},{6,7},{7,6},{8,9},{9,8},{10,11... | collective-permute-start | bytes 3080 | tf_op jit(solution)/shard_map/squares/ppermute | solution.py:31
  17.9 2.7 %collective-permute-done.1 = f32[256]{0:T(256)S(1)} collective-permute-done((f32[256]{0:T(256)S(1)}, f32[256]{0:T(256)S(1)}, u32[]{:S(2)}, u32[]{:S(2)}) %collective-permute-start.1) | collective-permute-done | bytes 1056 | tf_op jit(solution)/shard_map/squares/ppermute | solution.py:31
  20.6 0.0 collective-permute-done
  20.6 1.5 %broadcast_in_dim.10 = bf16[8,512,256]{2,1,0:T(8,128)(2,1)} broadcast(bf16[512,256]{1,0:T(8,128)(2,1)S(1)} %collective-permute-done), dimensions={1,2} | broadcast | bytes 2359296 | tf_op jit(solution)/shard_map/weight_gather/broadcast_in_dim | solution.py:193
  22.1 6.9 %collective-permute-start.2 = (bf16[256,4096]{1,0:T(8,128)(2,1)S(1)}, bf16[256,4096]{1,0:T(8,128)(2,1)}, u32[]{:S(2)}, u32[]{:S(2)}) collective-permute-start(bf16[256,4096]{1,0:T(8,128)(2,1)S(1)} %bitcast.28), channel_id=1, source_target_pairs={{0,2},{2,0},{1,3},{3,1},{4,6},{6,4},{5,7},{7,5},{8,10},{10,8},{9,1... | collective-permute-start | bytes 6291464 | tf_op jit(solution)/shard_map/core_swap/ppermute | solution.py:31
  29.0 4.4 %all-to-all-start = ((bf16[8,512,256]{2,1,0:T(8,128)(2,1)}), bf16[8,512,256]{2,1,0:T(8,128)(2,1)}, u32[]{:S(2)}, u32[]{:S(2)}) async-start(bf16[8,512,256]{2,1,0:T(8,128)(2,1)} %broadcast_in_dim.10), calls=%async_computation | async-start | bytes 4194304 | tf_op jit(solution)/shard_map/weight_gather/all_to_all | solution.py:195
  33.5 1.9 %collective-permute-start.3 = (f32[258,256]{1,0:T(8,128)S(1)}, f32[258,256]{1,0:T(8,128)S(1)}, u32[]{:S(2)}, u32[]{:S(2)}) collective-permute-start(f32[258,256]{1,0:T(8,128)S(1)} %pad_maximum_fusion.7), channel_id=1, source_target_pairs={{0,2},{2,0},{1,3},{3,1},{4,6},{6,4},{5,7},{7,5},{8,10},{10,8},{9,1... | collective-permute-start | bytes 792584 | tf_op jit(solution)/shard_map/core_swap/ppermute | solution.py:31
  35.4 1.5 %collective-permute-done.3 = f32[258,256]{1,0:T(8,128)S(1)} collective-permute-done((f32[258,256]{1,0:T(8,128)S(1)}, f32[258,256]{1,0:T(8,128)S(1)}, u32[]{:S(2)}, u32[]{:S(2)}) %collective-permute-start.3) | collective-permute-done | bytes 264224 | tf_op jit(solution)/shard_map/core_swap/ppermute | solution.py:31
  37.0 28.0 %all-to-all-done = bf16[8,512,256]{2,1,0:T(8,128)(2,1)} async-done(((bf16[8,512,256]{2,1,0:T(8,128)(2,1)}), bf16[8,512,256]{2,1,0:T(8,128)(2,1)}, u32[]{:S(2)}, u32[]{:S(2)}) %all-to-all-start) | async-done | bytes 2097184 | tf_op jit(solution)/shard_map/weight_gather/all_to_all | solution.py:195
  65.0 0.0 collective-permute-done.2
  65.0 3.5 %fusion.6 = (bf16[512,256]{1,0:T(8,128)(2,1)S(1)}, f32[512,256]{1,0:T(8,128)S(1)}) fusion(f32[256,256]{1,0:T(8,128)S(1)} %slice.13, f32[256,256]{1,0:T(8,128)S(1)} %bitcast_convert_fusion, f32[512]{0:T(512)S(1)} %get-tuple-element.32, bf16[4096,256]{1,0:T(8,128)(2,1)} %bitcast.3, bf16[256,4096]{1,0:T(8,128)(2,1)} %collective-permute-done.2, ...), kind=kOutput, calls=%fused_computation.18 | convolution fusion | flops 1082785792 | bytes 7604225 | tf_op jit(solution)/shard_map/keys/dot_general | solution.py:214
  68.5 1.9 %collective-permute-start.4 = (bf16[512,256]{1,0:T(8,128)(2,1)S(1)}, bf16[512,256]{1,0:T(8,128)(2,1)S(1)}, u32[]{:S(2)}, u32[]{:S(2)}) collective-permute-start(bf16[512,256]{1,0:T(8,128)(2,1)S(1)} %get-tuple-element.33), channel_id=1, source_target_pairs={{0,1},{1,0},{2,3},{3,2},{4,5},{5,4},{6,7},{7,6},{8,9},{9,8},{10,11... | collective-permute-start | bytes 786440 | tf_op jit(solution)/shard_map/keys/ppermute | solution.py:31
  70.4 8.5 %collective-permute-done.4 = bf16[512,256]{1,0:T(8,128)(2,1)S(1)} collective-permute-done((bf16[512,256]{1,0:T(8,128)(2,1)S(1)}, bf16[512,256]{1,0:T(8,128)(2,1)S(1)}, u32[]{:S(2)}, u32[]{:S(2)}) %collective-permute-start.4) | collective-permute-done | bytes 262176 | tf_op jit(solution)/shard_map/keys/ppermute | solution.py:31
  78.9 3.0 %convolution_convert_fusion = bf16[4096,256]{1,0:T(8,128)(2,1)S(1)} fusion(bf16[256,4096]{1,0:T(8,128)(2,1)} %collective-permute-done.2, bf16[256,4096]{1,0:T(8,128)(2,1)S(1)} %bitcast.30, f32[512,256]{1,0:T(8,128)S(1)} %get-tuple-element.34, bf16[512,256]{1,0:T(8,128)(2,1)S(1)} %collective-permute-done.4, f32[512]{0:T(512)S(1)} %get-tuple-element.31), kind=kOutput, calls=%fused_computation.1 | convolution fusion | flops 1083703296 | bytes 7079936 | tf_op jit(solution)/shard_map/gradient/dot_general | solution.py:221
  82.0 27.0 %all_to_all.21.terms = bf16[8,512,256]{2,1,0:T(8,128)(2,1)S(1)} all-to-all(bf16[8,512,256]{2,1,0:T(8,128)(2,1)S(1)} %bitcast.31), channel_id=1, replica_groups=mesh['worker'=16,'ylo'=2,'x'=4,'core'=2,'tensor'=2] {'x','ylo'}, dimensions={0} | all-to-all | bytes 4194304 | tf_op jit(solution)/shard_map/gradient/all_to_all | solution.py:224
  109.0 0.0 copy-start.4
  109.0 0.0 copy-start.5
  109.0 0.0 all-gather.2.cloned.1.call-done
  109.0 1.8 %sum_terms.1 = (bf16[512,256]{1,0:T(8,128)(2,1)}, f32[32,128]{1,0:T(8,128)}) custom-call(bf16[8,512,256]{2,1,0:T(8,128)(2,1)S(1)} %all_to_all.21.terms), custom_call_target="tpu_custom_call" | custom-call | bytes 2375680 | tf_op jit(solution)/shard_map/gradient/sum_terms/pallas_call | solution.py:44
  110.9 5.5 %collective-permute-start.5 = (bf16[512,256]{1,0:T(8,128)(2,1)}, bf16[512,256]{1,0:T(8,128)(2,1)S(1)}, u32[]{:S(2)}, u32[]{:S(2)}) collective-permute-start(bf16[512,256]{1,0:T(8,128)(2,1)} %get-tuple-element.22), channel_id=1, source_target_pairs={{0,0},{1,16},{2,1},{3,17},{4,4},{5,20},{6,5},{7,21},{8,8},{9,24},{... | collective-permute-start | bytes 786440 | tf_op jit(solution)/shard_map/gradient_home/ppermute | solution.py:31
  116.4 4.7 %all-to-all-start.2 = ((f32[32,1,128]{2,1,0:T(1,128)}), f32[32,1,128]{2,1,0:T(1,128)S(1)}, u32[]{:S(2)}, u32[]{:S(2)}) async-start(f32[32,1,128]{2,1,0:T(1,128)} %bitcast.12), calls=%async_computation.2 | async-start | bytes 32768 | tf_op jit(solution)/shard_map/norm/all_to_all | solution.py:232
  121.1 2.8 %convert_reduce_fusion.refs_9_ = f32[512,256]{1,0:T(8,128)S(1)} fusion(bf16[16,512,256]{2,1,0:T(8,128)(2,1)} %all-gather.2.cloned.1.call-done), kind=kLoop, calls=%fused_computation | loop fusion | flops 4063232 | bytes 4718592 | tf_op jit(solution)/shard_map/gradient/reduce_sum | solution.py:227
  123.9 4.0 %all-to-all-done.2 = f32[32,1,128]{2,1,0:T(1,128)S(1)} async-done(((f32[32,1,128]{2,1,0:T(1,128)}), f32[32,1,128]{2,1,0:T(1,128)S(1)}, u32[]{:S(2)}, u32[]{:S(2)}) %all-to-all-start.2) | async-done | bytes 16416 | tf_op jit(solution)/shard_map/norm/all_to_all | solution.py:232
  127.9 0.0 collective-permute-done.5.refs_3_
  127.9 2.9 %update.1 = (bf16[512,256]{1,0:T(8,128)(2,1)}, bf16[512,256]{1,0:T(8,128)(2,1)}, bf16[512,256]{1,0:T(8,128)(2,1)}, bf16[512,256]{1,0:T(8,128)(2,1)}, bf16[512,256]{1,0:T(8,128)(2,1)}) custom-call(s32[1]{0:T(128)} %bitcast.refs_0_, s32[4,4]{1,0:T(4,128)S(1)} %copy-done.5, f32[32,128]{1,0:T(8,128)S(1)} %bitcast.27, ...), custom_call_target="tpu_custom_call" | custom-call | bytes 3424324 | tf_op jit(solution)/shard_map/update/pallas_call | solution.py:44
  (21 shorter events, 0.1 us)
Async XLA Ops:
  7.2 14.9 %copy-start.6 = (bf16[1,256,4096]{2,1,0:T(8,128)(2,1)S(1)}, bf16[1,256,4096]{2,1,0:T(8,128)(2,1)}, u32[]{:S(2)}) copy-start(bf16[1,256,4096]{2,1,0:T(8,128)(2,1)} %param.11) | copy-start | bytes 6291460
  7.2 101.8 %all-gather.2.cloned.1.call-start = ((), (), s32[]{:S(2)}) async-start(), calls=%async_computation.3 | async-start | bytes 4456448 | tf_op jit(solution)/shard_map/outer_gather/all_gather | solution.py:211
  7.9 25.5 %copy-start.8 = (s32[1,256]{1,0:T(1,128)S(1)}, s32[1,256]{1,0:T(1,128)}, u32[]{:S(2)}) copy-start(s32[1,256]{1,0:T(1,128)} %param.10) | copy-start | bytes 3076
  7.9 25.5 %copy-start.7 = (bf16[1,256,256]{2,1,0:T(8,128)(2,1)S(1)}, bf16[1,256,256]{2,1,0:T(8,128)(2,1)}, u32[]{:S(2)}) copy-start(bf16[1,256,256]{2,1,0:T(8,128)(2,1)} %param.12) | copy-start | bytes 393220
  7.9 12.6 %collective-permute-start = (bf16[512,256]{1,0:T(8,128)(2,1)}, bf16[512,256]{1,0:T(8,128)(2,1)S(1)}, u32[]{:S(2)}, u32[]{:S(2)}) collective-permute-start(bf16[512,256]{1,0:T(8,128)(2,1)} %bitcast.23), channel_id=1, source_target_pairs={{0,0},{1,2},{2,16},{3,18},{4,4},{5,6},{6,20},{7,22},{8,8},{9,10},{... | collective-permute-start | bytes 786440 | tf_op jit(solution)/shard_map/weight_move/ppermute | solution.py:31
  14.8 5.8 %collective-permute-start.1 = (f32[256]{0:T(256)S(1)}, f32[256]{0:T(256)S(1)}, u32[]{:S(2)}, u32[]{:S(2)}) collective-permute-start(f32[256]{0:T(256)S(1)} %multiply_reduce_fusion), channel_id=1, source_target_pairs={{0,1},{1,0},{2,3},{3,2},{4,5},{5,4},{6,7},{7,6},{8,9},{9,8},{10,11... | collective-permute-start | bytes 3080 | tf_op jit(solution)/shard_map/squares/ppermute | solution.py:31
  22.1 42.9 %collective-permute-start.2 = (bf16[256,4096]{1,0:T(8,128)(2,1)S(1)}, bf16[256,4096]{1,0:T(8,128)(2,1)}, u32[]{:S(2)}, u32[]{:S(2)}) collective-permute-start(bf16[256,4096]{1,0:T(8,128)(2,1)S(1)} %bitcast.28), channel_id=1, source_target_pairs={{0,2},{2,0},{1,3},{3,1},{4,6},{6,4},{5,7},{7,5},{8,10},{10,8},{9,1... | collective-permute-start | bytes 6291464 | tf_op jit(solution)/shard_map/core_swap/ppermute | solution.py:31
  29.0 36.0 %all-to-all-start = ((bf16[8,512,256]{2,1,0:T(8,128)(2,1)}), bf16[8,512,256]{2,1,0:T(8,128)(2,1)}, u32[]{:S(2)}, u32[]{:S(2)}) async-start(bf16[8,512,256]{2,1,0:T(8,128)(2,1)} %broadcast_in_dim.10), calls=%async_computation | async-start | bytes 4194304 | tf_op jit(solution)/shard_map/weight_gather/all_to_all | solution.py:195
  33.5 3.4 %collective-permute-start.3 = (f32[258,256]{1,0:T(8,128)S(1)}, f32[258,256]{1,0:T(8,128)S(1)}, u32[]{:S(2)}, u32[]{:S(2)}) collective-permute-start(f32[258,256]{1,0:T(8,128)S(1)} %pad_maximum_fusion.7), channel_id=1, source_target_pairs={{0,2},{2,0},{1,3},{3,1},{4,6},{6,4},{5,7},{7,5},{8,10},{10,8},{9,1... | collective-permute-start | bytes 792584 | tf_op jit(solution)/shard_map/core_swap/ppermute | solution.py:31
  68.5 10.4 %collective-permute-start.4 = (bf16[512,256]{1,0:T(8,128)(2,1)S(1)}, bf16[512,256]{1,0:T(8,128)(2,1)S(1)}, u32[]{:S(2)}, u32[]{:S(2)}) collective-permute-start(bf16[512,256]{1,0:T(8,128)(2,1)S(1)} %get-tuple-element.33), channel_id=1, source_target_pairs={{0,1},{1,0},{2,3},{3,2},{4,5},{5,4},{6,7},{7,6},{8,9},{9,8},{10,11... | collective-permute-start | bytes 786440 | tf_op jit(solution)/shard_map/keys/ppermute | solution.py:31
  109.0 18.9 %copy-start = (bf16[1,512,256]{2,1,0:T(8,128)(2,1)S(1)}, bf16[1,512,256]{2,1,0:T(8,128)(2,1)}, u32[]{:S(2)}) copy-start(bf16[1,512,256]{2,1,0:T(8,128)(2,1)} %param.13) | copy-start | bytes 786436
  109.0 18.9 %copy-start.1 = (bf16[1,512,256]{2,1,0:T(8,128)(2,1)S(1)}, bf16[1,512,256]{2,1,0:T(8,128)(2,1)}, u32[]{:S(2)}) copy-start(bf16[1,512,256]{2,1,0:T(8,128)(2,1)} %param.14) | copy-start | bytes 786436
  109.0 18.9 %copy-start.2 = (bf16[1,512,256]{2,1,0:T(8,128)(2,1)S(1)}, bf16[1,512,256]{2,1,0:T(8,128)(2,1)}, u32[]{:S(2)}) copy-start(bf16[1,512,256]{2,1,0:T(8,128)(2,1)} %param.15) | copy-start | bytes 786436
  109.0 18.9 %copy-start.3 = (bf16[512,256]{1,0:T(8,128)(2,1)S(1)}, bf16[512,256]{1,0:T(8,128)(2,1)}, u32[]{:S(2)}) copy-start(bf16[512,256]{1,0:T(8,128)(2,1)} %refs_7_.1) | copy-start | bytes 786436
  109.0 18.9 %copy-start.4 = (bf16[512,256]{1,0:T(8,128)(2,1)S(1)}, bf16[512,256]{1,0:T(8,128)(2,1)}, u32[]{:S(2)}) copy-start(bf16[512,256]{1,0:T(8,128)(2,1)} %refs_8_.1) | copy-start | bytes 786436
  109.0 18.9 %copy-start.5 = (s32[4,4]{1,0:T(4,128)S(1)}, s32[4,4]{1,0:T(4,128)}, u32[]{:S(2)}) copy-start(s32[4,4]{1,0:T(4,128)} %refs_1_.1) | copy-start | bytes 196
  110.9 17.0 %collective-permute-start.5 = (bf16[512,256]{1,0:T(8,128)(2,1)}, bf16[512,256]{1,0:T(8,128)(2,1)S(1)}, u32[]{:S(2)}, u32[]{:S(2)}) collective-permute-start(bf16[512,256]{1,0:T(8,128)(2,1)} %get-tuple-element.22), channel_id=1, source_target_pairs={{0,0},{1,16},{2,1},{3,17},{4,4},{5,20},{6,5},{7,21},{8,8},{9,24},{... | collective-permute-start | bytes 786440 | tf_op jit(solution)/shard_map/gradient_home/ppermute | solution.py:31
  116.4 11.5 %all-to-all-start.2 = ((f32[32,1,128]{2,1,0:T(1,128)}), f32[32,1,128]{2,1,0:T(1,128)S(1)}, u32[]{:S(2)}, u32[]{:S(2)}) async-start(f32[32,1,128]{2,1,0:T(1,128)} %bitcast.12), calls=%async_computation.2 | async-start | bytes 32768 | tf_op jit(solution)/shard_map/norm/all_to_all | solution.py:232
Sparse Core Ops, SparseCore 0:
  10.1 75.7 all-gather.1

commit v3 on v2

--- a/solution.py
+++ b/solution.py
@@ -185,27 +185,25 @@
     with jax.named_scope("weight_move"):
         moved = permute(weight, PLANE, lambda yl, x, c, t: (c, x, t, yl))
 
-    with jax.named_scope("squares"):
-        squares = jnp.sum(jnp.square(mine.astype(F32)), axis=1)
-        squares = squares + swap(squares, "tensor")
-
     with jax.named_scope("weight_gather"):
         copies = jnp.broadcast_to(moved[None], (group, rows, cols))
-        copies, squares = lax.optimization_barrier((copies, squares))
         matrix = lax.all_to_all(copies, GROUP, 0, 0).reshape(group * rows, cols)
 
     with jax.named_scope("core_swap"):
-        inv = lax.rsqrt(squares / (2 * half) + 1e-05)
+        squares = jnp.sum(jnp.square(mine.astype(F32)), axis=1)
         mask = (token_ids[0] != 0).astype(F32)
         note = jnp.concatenate(
-            [targets[0].astype(F32), inv[None], mask[None]], axis=0
+            [targets[0].astype(F32), squares[None], mask[None]], axis=0
         )
-        note_other = swap(note, "core")
-        other = swap(after(mine, copies), "core")
-        both = jnp.concatenate([mine, other], axis=0)
+        note_other = swap(after(note, copies), "core")
+        ready = after(mine, copies)
+        other = [swap(ready[at : at + tokens // 2], "core") for at in (0, tokens // 2)]
+        both = jnp.concatenate([mine, *other], axis=0)
         target2 = jnp.concatenate([note[:tokens], note_other[:tokens]], axis=0)
-        inv2 = jnp.concatenate([note[tokens], note_other[tokens]])
+        squares2 = jnp.concatenate([note[tokens], note_other[tokens]])
         mask2 = jnp.concatenate([note[tokens + 1], note_other[tokens + 1]])
+        squares2 = squares2 + swap(squares2, "tensor")
+        inv2 = lax.rsqrt(squares2 / (2 * half) + 1e-05)
 
     with jax.named_scope("outer_gather"):
         deltas = lax.all_gather(prev_delta[0], WORKER)

time: 138 us -> 129 us (0.935); the launches traced: 138 us -> 126 us
  waiting for transfers between devices: 45.4 us -> 29.2 us
  local copies, waits for them, and re-layouts: 1.57 us -> 5.14 us
    all_to_all x1, waiting for transfers between devices: 28 us -> 11.4 us  [local(): matrix = lax.all_to_all(copies, GROUP, 0, 0).reshape(group * rows, cols)]
    slice x1 -> x2, local copies, waits for them, and re-layouts: 0.01 us -> 1.94 us  [the longest x1 1.16 us: local(): ready[at:at + tokens // 2]]
    slice x1, local copies, waits for them, and re-layouts: 0.02 us -> 1.67 us  [local(): target2 = jnp.concatenate([note[:tokens], note_other[:tokens]], axis=0)]
    ppermute x6 -> x7, waiting for transfers between devices: 12.7 us -> 13.2 us  [permute(): return lax.ppermute(value, axes if len(axes) > 1 else axes[0], pairs)]
    ppermute x6 -> x7, starting transfers between devices: 24.1 us -> 24.1 us  [permute(): return lax.ppermute(value, axes if len(axes) > 1 else axes[0], pairs)]
  transfers between devices with their start and end apart: 9 -> 10, of which waited for: 5 -> 6; matrix products, arithmetic and copies ran while one was open for 9% -> 14% of each run, Pallas kernels for 0% -> 0%
where the time goes in v3:
time: 129 us; the launch traced here: 126 us
  starting transfers between devices  34.2 us (27%)
  waiting for transfers between devices  29.2 us (23%)
  blocking collectives  26.1 us (20%)
  between operations  14.3 us (11%)
  matrix products  6.52 us (5%)
  other arithmetic  6.01 us (5%)
  local copies, waits for them, and re-layouts  5.14 us (4%)
  Pallas kernels  4.74 us (4%)
    all_to_all x1, blocking collectives, local(): terms = lax.all_to_all(term.reshape(group, rows, cols), GROUP, 0, 0)  26.1 us
    ppermute x7, starting transfers between devices, permute(): return lax.ppermute(value, axes if len(axes) > 1 else axes[0], pairs)  24.1 us
    ppermute x7, waiting for transfers between devices, permute(): return lax.ppermute(value, axes if len(axes) > 1 else axes[0], pairs)  13.2 us
    all_to_all x1, waiting for transfers between devices, local(): matrix = lax.all_to_all(copies, GROUP, 0, 0).reshape(group * rows, cols)  11.4 us
    all_to_all x1, starting transfers between devices, local(): partial = lax.all_to_all(partial, PLANE, 0, 0, tiled=True)  5.59 us
    pallas_call x2, Pallas kernels, call(): pl.pallas_call(kernel, grid=grid, in_specs=in_specs, out_specs=out_specs,...  4.74 us
    all_to_all x1, starting transfers between devices, local(): matrix = lax.all_to_all(copies, GROUP, 0, 0).reshape(group * rows, cols)  4.5 us
    all_to_all x1, waiting for transfers between devices, local(): partial = lax.all_to_all(partial, PLANE, 0, 0, tiled=True)  4 us
  transfers between devices with their start and end apart: 10, of which 6 were waited for; matrix products, arithmetic and copies ran while one was open for 14% of the time, Pallas kernels for 0%

profile of v3, /device:TPU:1, one launch (start us, length us, event | category | flops | bytes accessed | tf_op | source)
XLA Modules:
  0.0 126.3 jit_solution(12694498181892738255)
XLA Ops:
  7.2 0.0 all-gather.2.cloned.1.call-start
  7.2 0.7 all-gather.2.cloned.1.call-update
  7.9 4.6 %collective-permute-start = (bf16[512,256]{1,0:T(8,128)(2,1)}, bf16[512,256]{1,0:T(8,128)(2,1)S(1)}, u32[]{:S(2)}, u32[]{:S(2)}) collective-permute-start(bf16[512,256]{1,0:T(8,128)(2,1)} %bitcast.23), channel_id=1, source_target_pairs={{0,0},{1,2},{2,16},{3,18},{4,4},{5,6},{6,20},{7,22},{8,8},{9,10},{... | collective-permute-start | bytes 786440 | tf_op jit(solution)/shard_map/weight_move/ppermute | solution.py:31
  12.5 0.9 bitcast_convert_fusion
  13.4 0.0 copy-start.6
  13.4 2.2 %multiply_reduce_fusion = f32[256]{0:T(256)S(1)} fusion(bf16[1,256,4096]{2,1,0:T(8,128)(2,1)} %param.11), kind=kLoop, calls=%fused_computation.3 | loop fusion | flops 3145472 | bytes 2098176 | tf_op jit(solution)/shard_map/core_swap/reduce_sum | solution.py:193
  15.7 2.7 %collective-permute-done = bf16[512,256]{1,0:T(8,128)(2,1)S(1)} collective-permute-done((bf16[512,256]{1,0:T(8,128)(2,1)}, bf16[512,256]{1,0:T(8,128)(2,1)S(1)}, u32[]{:S(2)}, u32[]{:S(2)}) %collective-permute-start) | collective-permute-done | bytes 262176 | tf_op jit(solution)/shard_map/weight_move/ppermute | solution.py:31
  18.4 1.5 %broadcast_in_dim.10 = bf16[8,512,256]{2,1,0:T(8,128)(2,1)} broadcast(bf16[512,256]{1,0:T(8,128)(2,1)S(1)} %collective-permute-done), dimensions={1,2} | broadcast | bytes 2359296 | tf_op jit(solution)/shard_map/weight_gather/broadcast_in_dim | solution.py:189
  19.9 4.5 %all-to-all-start = ((bf16[8,512,256]{2,1,0:T(8,128)(2,1)}), bf16[8,512,256]{2,1,0:T(8,128)(2,1)}, u32[]{:S(2)}, u32[]{:S(2)}) async-start(bf16[8,512,256]{2,1,0:T(8,128)(2,1)} %broadcast_in_dim.10), calls=%async_computation | async-start | bytes 4194304 | tf_op jit(solution)/shard_map/weight_gather/all_to_all | solution.py:190
  24.4 1.2 fusion.5
  25.6 3.1 %collective-permute-start.1 = (bf16[128,4096]{1,0:T(8,128)(2,1)}, bf16[128,4096]{1,0:T(8,128)(2,1)}, u32[]{:S(2)}, u32[]{:S(2)}) collective-permute-start(bf16[128,4096]{1,0:T(8,128)(2,1)} %get-tuple-element.29), channel_id=1, source_target_pairs={{0,2},{2,0},{1,3},{3,1},{4,6},{6,4},{5,7},{7,5},{8,10},{10,8},{9,1... | collective-permute-start | bytes 3145736 | tf_op jit(solution)/shard_map/core_swap/ppermute | solution.py:31
  28.6 1.9 %collective-permute-start.2 = (bf16[128,4096]{1,0:T(8,128)(2,1)S(1)}, bf16[128,4096]{1,0:T(8,128)(2,1)}, u32[]{:S(2)}, u32[]{:S(2)}) collective-permute-start(bf16[128,4096]{1,0:T(8,128)(2,1)S(1)} %get-tuple-element.30), channel_id=1, source_target_pairs={{0,2},{2,0},{1,3},{3,1},{4,6},{6,4},{5,7},{7,5},{8,10},{10,8},{9,1... | collective-permute-start | bytes 3145736 | tf_op jit(solution)/shard_map/core_swap/ppermute | solution.py:31
  30.6 2.4 %collective-permute-start.3 = (f32[258,256]{1,0:T(8,128)S(1)}, f32[258,256]{1,0:T(8,128)}, u32[]{:S(2)}, u32[]{:S(2)}) collective-permute-start(f32[258,256]{1,0:T(8,128)S(1)} %pad_maximum_fusion.7), channel_id=1, source_target_pairs={{0,2},{2,0},{1,3},{3,1},{4,6},{6,4},{5,7},{7,5},{8,10},{10,8},{9,1... | collective-permute-start | bytes 792584 | tf_op jit(solution)/shard_map/core_swap/ppermute | solution.py:31
  33.0 1.3 %collective-permute-done.3 = f32[258,256]{1,0:T(8,128)} collective-permute-done((f32[258,256]{1,0:T(8,128)S(1)}, f32[258,256]{1,0:T(8,128)}, u32[]{:S(2)}, u32[]{:S(2)}) %collective-permute-start.3) | collective-permute-done | bytes 264224 | tf_op jit(solution)/shard_map/core_swap/ppermute | solution.py:31
  34.3 0.8 fusion.6
  35.1 4.7 %collective-permute-start.4 = (f32[512]{0:T(512)S(1)}, f32[512]{0:T(512)S(1)}, u32[]{:S(2)}, u32[]{:S(2)}) collective-permute-start(f32[512]{0:T(512)S(1)} %pad_maximum_fusion.8), channel_id=1, source_target_pairs={{0,1},{1,0},{2,3},{3,2},{4,5},{5,4},{6,7},{7,6},{8,9},{9,8},{10,11... | collective-permute-start | bytes 6152 | tf_op jit(solution)/shard_map/core_swap/ppermute | solution.py:31
  39.8 1.7 %slice.21 = f32[256,256]{1,0:T(8,128)} slice(f32[258,256]{1,0:T(8,128)} %collective-permute-done.3), slice={[0:256], [0:256]} | slice | bytes 524288 | tf_op jit(solution)/shard_map/core_swap/slice | solution.py:202
  41.5 1.7 %collective-permute-done.4 = f32[512]{0:T(512)S(1)} collective-permute-done((f32[512]{0:T(512)S(1)}, f32[512]{0:T(512)S(1)}, u32[]{:S(2)}, u32[]{:S(2)}) %collective-permute-start.4) | collective-permute-done | bytes 2080 | tf_op jit(solution)/shard_map/core_swap/ppermute | solution.py:31
  43.2 11.4 %all-to-all-done = bf16[8,512,256]{2,1,0:T(8,128)(2,1)} async-done(((bf16[8,512,256]{2,1,0:T(8,128)(2,1)}), bf16[8,512,256]{2,1,0:T(8,128)(2,1)}, u32[]{:S(2)}, u32[]{:S(2)}) %all-to-all-start) | async-done | bytes 2097184 | tf_op jit(solution)/shard_map/weight_gather/all_to_all | solution.py:190
  54.6 3.6 %fusion.7 = (bf16[512,256]{1,0:T(8,128)(2,1)S(1)}, f32[512,256]{1,0:T(8,128)S(1)}) fusion(f32[256,256]{1,0:T(8,128)} %slice.21, f32[256,256]{1,0:T(8,128)S(1)} %bitcast_convert_fusion, f32[512]{0:T(512)S(1)} %get-tuple-element.28, bf16[4096,256]{1,0:T(8,128)(2,1)} %bitcast.3, bf16[128,4096]{1,0:T(8,128)(2,1)} %collective-permute-done.2, ...), kind=kOutput, calls=%fused_computation.19 | convolution fusion | flops 1086980096 | bytes 7604225 | tf_op jit(solution)/shard_map/keys/dot_general | solution.py:212
  58.1 1.9 %collective-permute-start.5 = (bf16[512,256]{1,0:T(8,128)(2,1)S(1)}, bf16[512,256]{1,0:T(8,128)(2,1)S(1)}, u32[]{:S(2)}, u32[]{:S(2)}) collective-permute-start(bf16[512,256]{1,0:T(8,128)(2,1)S(1)} %get-tuple-element.33), channel_id=1, source_target_pairs={{0,1},{1,0},{2,3},{3,2},{4,5},{5,4},{6,7},{7,6},{8,9},{9,8},{10,11... | collective-permute-start | bytes 786440 | tf_op jit(solution)/shard_map/keys/ppermute | solution.py:31
  60.1 7.5 %collective-permute-done.5 = bf16[512,256]{1,0:T(8,128)(2,1)S(1)} collective-permute-done((bf16[512,256]{1,0:T(8,128)(2,1)S(1)}, bf16[512,256]{1,0:T(8,128)(2,1)S(1)}, u32[]{:S(2)}, u32[]{:S(2)}) %collective-permute-start.5) | collective-permute-done | bytes 262176 | tf_op jit(solution)/shard_map/keys/ppermute | solution.py:31
  67.6 3.0 %convolution_convert_fusion = bf16[4096,256]{1,0:T(8,128)(2,1)S(1)} fusion(bf16[128,4096]{1,0:T(8,128)(2,1)} %collective-permute-done.2, bf16[128,4096]{1,0:T(8,128)(2,1)} %collective-permute-done.1, bf16[256,4096]{1,0:T(8,128)(2,1)S(1)} %bitcast.30, f32[512,256]{1,0:T(8,128)S(1)} %get-tuple-element.34, bf16[512,256]{1,0:T(8,128)(2,1)S(1)} %collective-permute-done.5, ...), kind=kOutput, calls=%fused_computation.1 | convolution fusion | flops 1087897600 | bytes 7079936 | tf_op jit(solution)/shard_map/gradient/dot_general | solution.py:219
  70.5 26.1 %all_to_all.21.terms = bf16[8,512,256]{2,1,0:T(8,128)(2,1)S(1)} all-to-all(bf16[8,512,256]{2,1,0:T(8,128)(2,1)S(1)} %bitcast.31), channel_id=1, replica_groups=mesh['worker'=16,'ylo'=2,'x'=4,'core'=2,'tensor'=2] {'x','ylo'}, dimensions={0} | all-to-all | bytes 4194304 | tf_op jit(solution)/shard_map/gradient/all_to_all | solution.py:222
  96.7 0.0 copy-start.4
  96.7 0.0 all-gather.2.cloned.1.call-done
  96.7 1.8 %sum_terms.1 = (bf16[512,256]{1,0:T(8,128)(2,1)}, f32[32,128]{1,0:T(8,128)}) custom-call(bf16[8,512,256]{2,1,0:T(8,128)(2,1)S(1)} %all_to_all.21.terms), custom_call_target="tpu_custom_call" | custom-call | bytes 2375680 | tf_op jit(solution)/shard_map/gradient/sum_terms/pallas_call | solution.py:44
  98.6 5.5 %collective-permute-start.6 = (bf16[512,256]{1,0:T(8,128)(2,1)}, bf16[512,256]{1,0:T(8,128)(2,1)S(1)}, u32[]{:S(2)}, u32[]{:S(2)}) collective-permute-start(bf16[512,256]{1,0:T(8,128)(2,1)} %get-tuple-element.20), channel_id=1, source_target_pairs={{0,0},{1,16},{2,1},{3,17},{4,4},{5,20},{6,5},{7,21},{8,8},{9,24},{... | collective-permute-start | bytes 786440 | tf_op jit(solution)/shard_map/gradient_home/ppermute | solution.py:31
  104.0 5.6 %all-to-all-start.2 = ((f32[32,1,128]{2,1,0:T(1,128)}), f32[32,1,128]{2,1,0:T(1,128)S(1)}, u32[]{:S(2)}, u32[]{:S(2)}) async-start(f32[32,1,128]{2,1,0:T(1,128)} %bitcast.12), calls=%async_computation.2 | async-start | bytes 32768 | tf_op jit(solution)/shard_map/norm/all_to_all | solution.py:230
  109.6 2.8 %convert_reduce_fusion.refs_9_ = f32[512,256]{1,0:T(8,128)S(1)} fusion(bf16[16,512,256]{2,1,0:T(8,128)(2,1)} %all-gather.2.cloned.1.call-done), kind=kLoop, calls=%fused_computation | loop fusion | flops 4063232 | bytes 4718592 | tf_op jit(solution)/shard_map/gradient/reduce_sum | solution.py:225
  112.5 4.0 %all-to-all-done.2 = f32[32,1,128]{2,1,0:T(1,128)S(1)} async-done(((f32[32,1,128]{2,1,0:T(1,128)}), f32[32,1,128]{2,1,0:T(1,128)S(1)}, u32[]{:S(2)}, u32[]{:S(2)}) %all-to-all-start.2) | async-done | bytes 16416 | tf_op jit(solution)/shard_map/norm/all_to_all | solution.py:230
  116.5 2.9 %update.1 = (bf16[512,256]{1,0:T(8,128)(2,1)}, bf16[512,256]{1,0:T(8,128)(2,1)}, bf16[512,256]{1,0:T(8,128)(2,1)}, bf16[512,256]{1,0:T(8,128)(2,1)}, bf16[512,256]{1,0:T(8,128)(2,1)}) custom-call(s32[1]{0:T(128)} %bitcast.refs_0_, s32[4,4]{1,0:T(4,128)S(1)} %copy-done.5, f32[32,128]{1,0:T(8,128)S(1)} %bitcast.27, ...), custom_call_target="tpu_custom_call" | custom-call | bytes 3424324 | tf_op jit(solution)/shard_map/update/pallas_call | solution.py:44
  (21 shorter events, 0.1 us)
Async XLA Ops:
  7.2 89.6 %all-gather.2.cloned.1.call-start = ((), (), s32[]{:S(2)}) async-start(), calls=%async_computation.3 | async-start | bytes 4456448 | tf_op jit(solution)/shard_map/outer_gather/all_gather | solution.py:209
  7.9 10.5 %collective-permute-start = (bf16[512,256]{1,0:T(8,128)(2,1)}, bf16[512,256]{1,0:T(8,128)(2,1)S(1)}, u32[]{:S(2)}, u32[]{:S(2)}) collective-permute-start(bf16[512,256]{1,0:T(8,128)(2,1)} %bitcast.23), channel_id=1, source_target_pairs={{0,0},{1,2},{2,16},{3,18},{4,4},{5,6},{6,20},{7,22},{8,8},{9,10},{... | collective-permute-start | bytes 786440 | tf_op jit(solution)/shard_map/weight_move/ppermute | solution.py:31
  13.4 11.0 %copy-start.6 = (bf16[1,256,4096]{2,1,0:T(8,128)(2,1)S(1)}, bf16[1,256,4096]{2,1,0:T(8,128)(2,1)}, u32[]{:S(2)}) copy-start(bf16[1,256,4096]{2,1,0:T(8,128)(2,1)} %param.11) | copy-start | bytes 6291460
  19.9 10.7 %copy-start.7 = (s32[1,256]{1,0:T(1,128)S(1)}, s32[1,256]{1,0:T(1,128)}, u32[]{:S(2)}) copy-start(s32[1,256]{1,0:T(1,128)} %param.10) | copy-start | bytes 3076
  19.9 34.7 %all-to-all-start = ((bf16[8,512,256]{2,1,0:T(8,128)(2,1)}), bf16[8,512,256]{2,1,0:T(8,128)(2,1)}, u32[]{:S(2)}, u32[]{:S(2)}) async-start(bf16[8,512,256]{2,1,0:T(8,128)(2,1)} %broadcast_in_dim.10), calls=%async_computation | async-start | bytes 4194304 | tf_op jit(solution)/shard_map/weight_gather/all_to_all | solution.py:190
  25.6 17.6 %collective-permute-start.1 = (bf16[128,4096]{1,0:T(8,128)(2,1)}, bf16[128,4096]{1,0:T(8,128)(2,1)}, u32[]{:S(2)}, u32[]{:S(2)}) collective-permute-start(bf16[128,4096]{1,0:T(8,128)(2,1)} %get-tuple-element.29), channel_id=1, source_target_pairs={{0,2},{2,0},{1,3},{3,1},{4,6},{6,4},{5,7},{7,5},{8,10},{10,8},{9,1... | collective-permute-start | bytes 3145736 | tf_op jit(solution)/shard_map/core_swap/ppermute | solution.py:31
  28.6 14.5 %collective-permute-start.2 = (bf16[128,4096]{1,0:T(8,128)(2,1)S(1)}, bf16[128,4096]{1,0:T(8,128)(2,1)}, u32[]{:S(2)}, u32[]{:S(2)}) collective-permute-start(bf16[128,4096]{1,0:T(8,128)(2,1)S(1)} %get-tuple-element.30), channel_id=1, source_target_pairs={{0,2},{2,0},{1,3},{3,1},{4,6},{6,4},{5,7},{7,5},{8,10},{10,8},{9,1... | collective-permute-start | bytes 3145736 | tf_op jit(solution)/shard_map/core_swap/ppermute | solution.py:31
  30.6 3.7 %collective-permute-start.3 = (f32[258,256]{1,0:T(8,128)S(1)}, f32[258,256]{1,0:T(8,128)}, u32[]{:S(2)}, u32[]{:S(2)}) collective-permute-start(f32[258,256]{1,0:T(8,128)S(1)} %pad_maximum_fusion.7), channel_id=1, source_target_pairs={{0,2},{2,0},{1,3},{3,1},{4,6},{6,4},{5,7},{7,5},{8,10},{10,8},{9,1... | collective-permute-start | bytes 792584 | tf_op jit(solution)/shard_map/core_swap/ppermute | solution.py:31
  35.1 8.0 %collective-permute-start.4 = (f32[512]{0:T(512)S(1)}, f32[512]{0:T(512)S(1)}, u32[]{:S(2)}, u32[]{:S(2)}) collective-permute-start(f32[512]{0:T(512)S(1)} %pad_maximum_fusion.8), channel_id=1, source_target_pairs={{0,1},{1,0},{2,3},{3,2},{4,5},{5,4},{6,7},{7,6},{8,9},{9,8},{10,11... | collective-permute-start | bytes 6152 | tf_op jit(solution)/shard_map/core_swap/ppermute | solution.py:31
  58.1 9.4 %collective-permute-start.5 = (bf16[512,256]{1,0:T(8,128)(2,1)S(1)}, bf16[512,256]{1,0:T(8,128)(2,1)S(1)}, u32[]{:S(2)}, u32[]{:S(2)}) collective-permute-start(bf16[512,256]{1,0:T(8,128)(2,1)S(1)} %get-tuple-element.33), channel_id=1, source_target_pairs={{0,1},{1,0},{2,3},{3,2},{4,5},{5,4},{6,7},{7,6},{8,9},{9,8},{10,11... | collective-permute-start | bytes 786440 | tf_op jit(solution)/shard_map/keys/ppermute | solution.py:31
  96.7 19.8 %copy-start = (bf16[1,512,256]{2,1,0:T(8,128)(2,1)S(1)}, bf16[1,512,256]{2,1,0:T(8,128)(2,1)}, u32[]{:S(2)}) copy-start(bf16[1,512,256]{2,1,0:T(8,128)(2,1)} %param.13) | copy-start | bytes 786436
  96.7 19.8 %copy-start.1 = (bf16[1,512,256]{2,1,0:T(8,128)(2,1)S(1)}, bf16[1,512,256]{2,1,0:T(8,128)(2,1)}, u32[]{:S(2)}) copy-start(bf16[1,512,256]{2,1,0:T(8,128)(2,1)} %param.14) | copy-start | bytes 786436
  96.7 19.8 %copy-start.2 = (bf16[1,512,256]{2,1,0:T(8,128)(2,1)S(1)}, bf16[1,512,256]{2,1,0:T(8,128)(2,1)}, u32[]{:S(2)}) copy-start(bf16[1,512,256]{2,1,0:T(8,128)(2,1)} %param.15) | copy-start | bytes 786436
  96.7 19.8 %copy-start.3 = (bf16[512,256]{1,0:T(8,128)(2,1)S(1)}, bf16[512,256]{1,0:T(8,128)(2,1)}, u32[]{:S(2)}) copy-start(bf16[512,256]{1,0:T(8,128)(2,1)} %refs_7_.1) | copy-start | bytes 786436
  96.7 19.8 %copy-start.4 = (bf16[512,256]{1,0:T(8,128)(2,1)S(1)}, bf16[512,256]{1,0:T(8,128)(2,1)}, u32[]{:S(2)}) copy-start(bf16[512,256]{1,0:T(8,128)(2,1)} %refs_8_.1) | copy-start | bytes 786436
  96.7 19.8 %copy-start.5 = (s32[4,4]{1,0:T(4,128)S(1)}, s32[4,4]{1,0:T(4,128)}, u32[]{:S(2)}) copy-start(s32[4,4]{1,0:T(4,128)} %refs_1_.1) | copy-start | bytes 196
  98.6 17.9 %collective-permute-start.6 = (bf16[512,256]{1,0:T(8,128)(2,1)}, bf16[512,256]{1,0:T(8,128)(2,1)S(1)}, u32[]{:S(2)}, u32[]{:S(2)}) collective-permute-start(bf16[512,256]{1,0:T(8,128)(2,1)} %get-tuple-element.20), channel_id=1, source_target_pairs={{0,0},{1,16},{2,1},{3,17},{4,4},{5,20},{6,5},{7,21},{8,8},{9,24},{... | collective-permute-start | bytes 786440 | tf_op jit(solution)/shard_map/gradient_home/ppermute | solution.py:31
  104.0 12.4 %all-to-all-start.2 = ((f32[32,1,128]{2,1,0:T(1,128)}), f32[32,1,128]{2,1,0:T(1,128)S(1)}, u32[]{:S(2)}, u32[]{:S(2)}) async-start(f32[32,1,128]{2,1,0:T(1,128)} %bitcast.12), calls=%async_computation.2 | async-start | bytes 32768 | tf_op jit(solution)/shard_map/norm/all_to_all | solution.py:230
Sparse Core Ops, SparseCore 0:
  10.1 75.8 all-gather.1

commit v4 on v3

--- a/solution.py
+++ b/solution.py
@@ -1,3 +1,5 @@
+import itertools
+
 import jax
 import jax.numpy as jnp
 from jax import lax
@@ -19,7 +21,7 @@
 }
 BF = jnp.bfloat16
 F32 = jnp.float32
-VMEM_LIMIT = 32 * 2**20
+VMEM_LIMIT = 8 * 2**20
 
 
 def permute(value, axes, move):
@@ -39,7 +41,7 @@
     return lax.optimization_barrier((value, *others))[0]
 
 
-def call(kernel, name, grid, ins, in_specs, outs, out_specs, scratch=(), flops=0):
+def call(kernel, name, grid, ins, in_specs, outs, out_specs, scratch=(), flops=0, vmem=VMEM_LIMIT):
     moved = sum(a.size * a.dtype.itemsize for a in (*ins, *outs))
     return pl.pallas_call(
         kernel,
@@ -49,13 +51,56 @@
         out_shape=outs,
         scratch_shapes=scratch,
         name=name,
-        compiler_params=pltpu.CompilerParams(vmem_limit_bytes=VMEM_LIMIT),
+        compiler_params=pltpu.CompilerParams(vmem_limit_bytes=vmem),
         cost_estimate=pl.CostEstimate(
             flops=flops, bytes_accessed=moved, transcendentals=0
         ),
     )(*ins)
 
 
+def keys_kernel(both, matrix, scale, target, part, low, total):
+    step = pl.program_id(0)
+    value = jnp.dot(both[...], matrix[...], preferred_element_type=F32)
+
+    @pl.when(step == 0)
+    def _():
+        total[...] = value
+
+    @pl.when(step == 1)
+    def _():
+        keys = (total[...] + value) * scale[...] - target[...]
+        part[...] = keys
+        low[...] = keys.astype(BF)
+
+
+def partial_keys(both, matrix, scale, target):
+    tokens, half = both.shape
+    cols = matrix.shape[1]
+    depth = half // 2
+    outs = [
+        jax.ShapeDtypeStruct((tokens, cols), F32),
+        jax.ShapeDtypeStruct((tokens, cols), BF),
+    ]
+    full = pl.BlockSpec((tokens, cols), lambda k: (0, 0))
+    return call(
+        keys_kernel,
+        "partial_keys",
+        (2,),
+        (both, matrix, scale, target),
+        [
+            pl.BlockSpec((tokens, depth), lambda k: (0, k)),
+            pl.BlockSpec((depth, cols), lambda k: (k, 0)),
+            full,
+            full,
+        ],
+        outs,
+        [full, full],
+        [pltpu.VMEM((tokens, cols), F32)],
+        2 * tokens * half * cols,
+        48 * 2**20,
+    )
+
+
 def sum_kernel(terms, total, squares, so_far):
     step = pl.program_id(0)
     value = jnp.sum(terms[...].astype(F32), axis=0)
@@ -74,7 +119,7 @@
 
 def sum_terms(terms, places):
     group, rows, cols = terms.shape
-    part = rows // 4
+    part = rows // 2
     return call(
         sum_kernel,
         "sum_terms",
@@ -115,8 +160,9 @@
     norm = jnp.sqrt(jnp.sum(squares[...], axis=0, keepdims=True)[:, :1])
     clip = jnp.minimum(1.0, 1.0 / (norm + 1e-06))
     heads = raw.shape[1] // HD
-    for head in range(heads):
-        at = (slice(None), slice(head * HD, (head + 1) * HD))
+    tiles = raw.shape[0] // HD
+    for tile, head in itertools.product(range(tiles), range(heads)):
+        at = (slice(tile * HD, (tile + 1) * HD), slice(head * HD, (head + 1) * HD))
         clipped = raw[at].astype(F32) * clip
         first = 0.9 * adam_first[at].astype(F32) + 0.1 * clipped
         second = 0.95 * adam_second[at].astype(F32) + 0.05 * clipped * clipped
@@ -124,7 +170,7 @@
         stepped = old - 0.0004 * (first / (jnp.sqrt(second) + 1e-08) + 0.1 * old)
         new_first[at] = first.astype(BF)
         new_second[at] = second.astype(BF)
-        chosen = fragment[step, spot[0] * heads + head] == 0
+        chosen = fragment[step * tiles + tile, spot[0] * heads + head] == 0
 
         @pl.when(chosen)
         def _():
@@ -147,12 +193,12 @@
 
 def update(replicas, spot, fragment, squares, arrays):
     rows, cols = arrays[0].shape
-    block = pl.BlockSpec((HD, cols), lambda k: (k, 0))
+    block = pl.BlockSpec((rows // 2, cols), lambda k: (k, 0))
     smem = pl.BlockSpec(memory_space=pltpu.SMEM)
     return call(
         lambda *refs: update_kernel(replicas, *refs),
         "update",
-        (rows // HD,),
+        (2,),
         (spot, fragment, squares, *arrays),
         [smem, smem, pl.BlockSpec(squares.shape, lambda k: (0, 0))]
         + [block] * len(arrays),
@@ -209,9 +255,14 @@
         deltas = lax.all_gather(prev_delta[0], WORKER)
 
     with jax.named_scope("keys"):
-        part = jnp.dot(both, matrix, preferred_element_type=F32) * inv2[:, None]
-        part = jnp.where(core == side, part - target2, part)
-        theirs = swap(part.astype(BF), "tensor")
+        shape = (2 * tokens, cols)
+        spread = jnp.broadcast_to(inv2[:, None], shape)
+        shift = jnp.where(core == side, target2, 0.0)
+        both, spread, shift, matrix = lax.optimization_barrier(
+            (both, spread, shift, matrix)
+        )
+        part, low = partial_keys(both, matrix, spread, shift)
+        theirs = swap(low, "tensor")
         scale = (inv2 * mask2)[:, None]
         resid = ((part + theirs.astype(F32)) * scale).astype(BF)
 

time: 129 us -> 125 us (0.969); the launches traced: 126 us -> 125 us
  matrix products: 6.52 us -> 1.4 us
  waiting for transfers between devices: 29.2 us -> 24.6 us
  other arithmetic: 6.01 us -> 10.5 us
  Pallas kernels: 4.74 us -> 7.13 us
  blocking collectives: 26.1 us -> 28 us
    concatenate x0 -> x1, other arithmetic: none -> 3.86 us  [local(): both = jnp.concatenate([mine, *other], axis=0)]
    all_to_all x1, waiting for transfers between devices: 11.4 us -> 7.62 us  [local(): matrix = lax.all_to_all(copies, GROUP, 0, 0).reshape(group * rows, cols)]
    dot_general x1 -> x0, matrix products: 3.56 us -> none  [local(): part = jnp.dot(both, matrix, preferred_element_type=F32) * inv2[:, None]]
    ppermute x7, starting transfers between devices: 24.1 us -> 26.5 us  [permute(): return lax.ppermute(value, axes if len(axes) > 1 else axes[0], pairs)]
    pallas_call x2 -> x3, Pallas kernels: 4.74 us -> 7.13 us  [call(): pl.pallas_call(kernel, grid=grid, in_specs=in_specs, out_specs=out_specs,...]
    all_to_all x1, starting transfers between devices: 5.59 us -> 3.63 us  [local(): partial = lax.all_to_all(partial, PLANE, 0, 0, tiled=True)]
    slice x1, local copies, waits for them, and re-layouts: 1.16 us -> 3.11 us  [local(): ready[at:at + tokens // 2]]
    all_to_all x1, blocking collectives: 26.1 us -> 28 us  [local(): terms = lax.all_to_all(term.reshape(group, rows, cols), GROUP, 0, 0)]
  transfers between devices with their start and end apart: 10 -> 10, of which waited for: 6 -> 6; matrix products, arithmetic and copies ran while one was open for 14% -> 13% of each run, Pallas kernels for 0% -> 3%
where the time goes in v4:
time: 125 us
  starting transfers between devices  34.2 us (27%)
  blocking collectives  28 us (22%)
  waiting for transfers between devices  24.6 us (20%)
  between operations  14.2 us (11%)
  other arithmetic  10.5 us (8%)
  Pallas kernels  7.13 us (6%)
  local copies, waits for them, and re-layouts  4.82 us (4%)
  matrix products  1.4 us (1%)
    all_to_all x1, blocking collectives, local(): terms = lax.all_to_all(term.reshape(group, rows, cols), GROUP, 0, 0)  28 us
    ppermute x7, starting transfers between devices, permute(): return lax.ppermute(value, axes if len(axes) > 1 else axes[0], pairs)  26.5 us
    ppermute x7, waiting for transfers between devices, permute(): return lax.ppermute(value, axes if len(axes) > 1 else axes[0], pairs)  12.5 us
    all_to_all x1, waiting for transfers between devices, local(): matrix = lax.all_to_all(copies, GROUP, 0, 0).reshape(group * rows, cols)  7.62 us
    pallas_call x3, Pallas kernels, call(): pl.pallas_call(kernel, grid=grid, in_specs=in_specs, out_specs=out_specs,...  7.13 us
    all_to_all x1, starting transfers between devices, local(): matrix = lax.all_to_all(copies, GROUP, 0, 0).reshape(group * rows, cols)  4.02 us
    concatenate x1, other arithmetic, local(): both = jnp.concatenate([mine, *other], axis=0)  3.86 us
    all_to_all x1, waiting for transfers between devices, local(): partial = lax.all_to_all(partial, PLANE, 0, 0, tiled=True)  3.73 us
  transfers between devices with their start and end apart: 10, of which 6 were waited for; matrix products, arithmetic and copies ran while one was open for 13% of the time, Pallas kernels for 3%

profile of v4, /device:TPU:1, one launch (start us, length us, event | category | flops | bytes accessed | tf_op | source)
XLA Modules:
  0.0 124.9 jit_solution(10034485851733634826)
XLA Ops:
  7.2 0.0 all-gather.2.cloned.1.call-start
  7.2 0.7 all-gather.2.cloned.1.call-update
  7.9 4.6 %collective-permute-start = (bf16[512,256]{1,0:T(8,128)(2,1)}, bf16[512,256]{1,0:T(8,128)(2,1)S(1)}, u32[]{:S(2)}, u32[]{:S(2)}) collective-permute-start(bf16[512,256]{1,0:T(8,128)(2,1)} %bitcast.24), channel_id=1, source_target_pairs={{0,0},{1,2},{2,16},{3,18},{4,4},{5,6},{6,20},{7,22},{8,8},{9,10},{... | collective-permute-start | bytes 786440 | tf_op jit(solution)/shard_map/weight_move/ppermute | solution.py:33
  12.5 0.9 bitcast_convert_fusion
  13.4 0.7 compare_convert_fusion
  14.1 2.1 %multiply_reduce_fusion = f32[256]{0:T(256)S(1)} fusion(bf16[1,256,4096]{2,1,0:T(8,128)(2,1)} %param.11), kind=kLoop, calls=%fused_computation.3 | loop fusion | flops 3145472 | bytes 2098176 | tf_op jit(solution)/shard_map/core_swap/reduce_sum | solution.py:239
  16.2 2.2 %collective-permute-done = bf16[512,256]{1,0:T(8,128)(2,1)S(1)} collective-permute-done((bf16[512,256]{1,0:T(8,128)(2,1)}, bf16[512,256]{1,0:T(8,128)(2,1)S(1)}, u32[]{:S(2)}, u32[]{:S(2)}) %collective-permute-start) | collective-permute-done | bytes 262176 | tf_op jit(solution)/shard_map/weight_move/ppermute | solution.py:33
  18.4 1.5 %broadcast_in_dim.30 = bf16[8,512,256]{2,1,0:T(8,128)(2,1)} broadcast(bf16[512,256]{1,0:T(8,128)(2,1)S(1)} %collective-permute-done), dimensions={1,2} | broadcast | bytes 2359296 | tf_op jit(solution)/shard_map/weight_gather/broadcast_in_dim | solution.py:235
  19.9 4.0 %all-to-all-start = ((bf16[8,512,256]{2,1,0:T(8,128)(2,1)}), bf16[8,512,256]{2,1,0:T(8,128)(2,1)S(1)}, u32[]{:S(2)}, u32[]{:S(2)}) async-start(bf16[8,512,256]{2,1,0:T(8,128)(2,1)} %broadcast_in_dim.30), calls=%async_computation | async-start | bytes 4194304 | tf_op jit(solution)/shard_map/weight_gather/all_to_all | solution.py:236
  23.9 3.1 %fusion.1 = (bf16[128,4096]{1,0:T(8,128)(2,1)}, bf16[128,4096]{1,0:T(8,128)(2,1)}) fusion(bf16[256,4096]{1,0:T(8,128)(2,1)} %bitcast.29), kind=kLoop, calls=%fused_computation.13 | loop fusion | bytes 4194304 | tf_op jit(solution)/shard_map/core_swap/slice | solution.py:246
  27.0 3.2 %collective-permute-start.1 = (bf16[128,4096]{1,0:T(8,128)(2,1)}, bf16[128,4096]{1,0:T(8,128)(2,1)}, u32[]{:S(2)}, u32[]{:S(2)}) collective-permute-start(bf16[128,4096]{1,0:T(8,128)(2,1)} %get-tuple-element.41), channel_id=1, source_target_pairs={{0,2},{2,0},{1,3},{3,1},{4,6},{6,4},{5,7},{7,5},{8,10},{10,8},{9,1... | collective-permute-start | bytes 3145736 | tf_op jit(solution)/shard_map/core_swap/ppermute | solution.py:33
  30.2 1.9 %collective-permute-start.2 = (bf16[128,4096]{1,0:T(8,128)(2,1)}, bf16[128,4096]{1,0:T(8,128)(2,1)}, u32[]{:S(2)}, u32[]{:S(2)}) collective-permute-start(bf16[128,4096]{1,0:T(8,128)(2,1)} %get-tuple-element.42), channel_id=1, source_target_pairs={{0,2},{2,0},{1,3},{3,1},{4,6},{6,4},{5,7},{7,5},{8,10},{10,8},{9,1... | collective-permute-start | bytes 3145736 | tf_op jit(solution)/shard_map/core_swap/ppermute | solution.py:33
  32.2 2.4 %collective-permute-start.3 = (f32[258,256]{1,0:T(8,128)S(1)}, f32[258,256]{1,0:T(8,128)S(1)}, u32[]{:S(2)}, u32[]{:S(2)}) collective-permute-start(f32[258,256]{1,0:T(8,128)S(1)} %pad_maximum_fusion.1), channel_id=1, source_target_pairs={{0,2},{2,0},{1,3},{3,1},{4,6},{6,4},{5,7},{7,5},{8,10},{10,8},{9,1... | collective-permute-start | bytes 792584 | tf_op jit(solution)/shard_map/core_swap/ppermute | solution.py:33
  34.6 1.1 collective-permute-done.3
  35.8 5.0 %collective-permute-start.4 = (f32[512]{0:T(512)S(1)}, f32[512]{0:T(512)S(1)}, u32[]{:S(2)}, u32[]{:S(2)}) collective-permute-start(f32[512]{0:T(512)S(1)} %pad_maximum_fusion.2), channel_id=1, source_target_pairs={{0,1},{1,0},{2,3},{3,2},{4,5},{5,4},{6,7},{7,6},{8,9},{9,8},{10,11... | collective-permute-start | bytes 6152 | tf_op jit(solution)/shard_map/core_swap/ppermute | solution.py:33
  40.8 1.7 %collective-permute-done.4 = f32[512]{0:T(512)S(1)} collective-permute-done((f32[512]{0:T(512)S(1)}, f32[512]{0:T(512)S(1)}, u32[]{:S(2)}, u32[]{:S(2)}) %collective-permute-start.4) | collective-permute-done | bytes 2080 | tf_op jit(solution)/shard_map/core_swap/ppermute | solution.py:33
  42.6 3.9 %pad_maximum_fusion.both = bf16[512,4096]{1,0:T(8,128)(2,1)} fusion(bf16[128,4096]{1,0:T(8,128)(2,1)} %collective-permute-done.2, bf16[128,4096]{1,0:T(8,128)(2,1)} %collective-permute-done.1, bf16[256,4096]{1,0:T(8,128)(2,1)} %bitcast.30), kind=kLoop, calls=%fused_computation.2 | loop fusion | flops 12582912 | bytes 8388608 | tf_op jit(solution)/shard_map/core_swap/concatenate | solution.py:247
  46.4 7.6 %all-to-all-done = bf16[8,512,256]{2,1,0:T(8,128)(2,1)S(1)} async-done(((bf16[8,512,256]{2,1,0:T(8,128)(2,1)}), bf16[8,512,256]{2,1,0:T(8,128)(2,1)S(1)}, u32[]{:S(2)}, u32[]{:S(2)}) %all-to-all-start) | async-done | bytes 2097184 | tf_op jit(solution)/shard_map/weight_gather/all_to_all | solution.py:236
  54.0 0.1 broadcast_in_dim.32.scale
  54.2 3.3 %partial_keys.1 = (f32[512,256]{1,0:T(8,128)S(1)}, bf16[512,256]{1,0:T(8,128)(2,1)S(1)}) custom-call(bf16[512,4096]{1,0:T(8,128)(2,1)} %pad_maximum_fusion.both, bf16[4096,256]{1,0:T(8,128)(2,1)S(1)} %bitcast.23, f32[512,256]{1,0:T(8,128)S(1)} %broadcast_in_dim.32.scale, f32[512,256]{1,0:T(8,128)S(1)} %maximum_select_fusion.target), custom_call_target="tpu_custom_call" | custom-call | flops 1073741824 | bytes 8126464 | tf_op jit(solution)/shard_map/keys/partial_keys/pallas_call | solution.py:46
  57.5 1.9 %collective-permute-start.5 = (bf16[512,256]{1,0:T(8,128)(2,1)S(1)}, bf16[512,256]{1,0:T(8,128)(2,1)S(1)}, u32[]{:S(2)}, u32[]{:S(2)}) collective-permute-start(bf16[512,256]{1,0:T(8,128)(2,1)S(1)} %get-tuple-element.29), channel_id=1, source_target_pairs={{0,1},{1,0},{2,3},{3,2},{4,5},{5,4},{6,7},{7,6},{8,9},{9,8},{10,11... | collective-permute-start | bytes 786440 | tf_op jit(solution)/shard_map/keys/ppermute | solution.py:33
  59.4 7.5 %collective-permute-done.5 = bf16[512,256]{1,0:T(8,128)(2,1)S(1)} collective-permute-done((bf16[512,256]{1,0:T(8,128)(2,1)S(1)}, bf16[512,256]{1,0:T(8,128)(2,1)S(1)}, u32[]{:S(2)}, u32[]{:S(2)}) %collective-permute-start.5) | collective-permute-done | bytes 262176 | tf_op jit(solution)/shard_map/keys/ppermute | solution.py:33
  67.0 1.4 %convolution_convert_fusion = bf16[4096,256]{1,0:T(8,128)(2,1)S(1)} fusion(bf16[512,4096]{1,0:T(8,128)(2,1)S(1)} %copy-done.6, f32[512,256]{1,0:T(8,128)S(1)} %get-tuple-element.28, bf16[512,256]{1,0:T(8,128)(2,1)S(1)} %collective-permute-done.5, f32[512]{0:T(512)S(1)} %get-tuple-element.39), kind=kOutput, calls=%fused_computation.1 | convolution fusion | flops 1075314688 | bytes 7079936 | tf_op jit(solution)/shard_map/gradient/dot_general | solution.py:270
  68.4 28.0 %all_to_all.21.terms = bf16[8,512,256]{2,1,0:T(8,128)(2,1)S(1)} all-to-all(bf16[8,512,256]{2,1,0:T(8,128)(2,1)S(1)} %bitcast.31), channel_id=1, replica_groups=mesh['worker'=16,'ylo'=2,'x'=4,'core'=2,'tensor'=2] {'x','ylo'}, dimensions={0} | all-to-all | bytes 4194304 | tf_op jit(solution)/shard_map/gradient/all_to_all | solution.py:273
  96.4 0.0 copy-start.5
  96.4 0.0 all-gather.2.cloned.1.call-done
  96.5 1.3 %sum_terms.1 = (bf16[512,256]{1,0:T(8,128)(2,1)}, f32[32,128]{1,0:T(8,128)}) custom-call(bf16[8,512,256]{2,1,0:T(8,128)(2,1)S(1)} %all_to_all.21.terms), custom_call_target="tpu_custom_call" | custom-call | bytes 2375680 | tf_op jit(solution)/shard_map/gradient/sum_terms/pallas_call | solution.py:46
  97.8 7.5 %collective-permute-start.6 = (bf16[512,256]{1,0:T(8,128)(2,1)}, bf16[512,256]{1,0:T(8,128)(2,1)S(1)}, u32[]{:S(2)}, u32[]{:S(2)}) collective-permute-start(bf16[512,256]{1,0:T(8,128)(2,1)} %get-tuple-element.32), channel_id=1, source_target_pairs={{0,0},{1,16},{2,1},{3,17},{4,4},{5,20},{6,5},{7,21},{8,8},{9,24},{... | collective-permute-start | bytes 786440 | tf_op jit(solution)/shard_map/gradient_home/ppermute | solution.py:33
  105.3 3.6 %all-to-all-start.2 = ((f32[32,1,128]{2,1,0:T(1,128)}), f32[32,1,128]{2,1,0:T(1,128)S(1)}, u32[]{:S(2)}, u32[]{:S(2)}) async-start(f32[32,1,128]{2,1,0:T(1,128)} %bitcast.12), calls=%async_computation.2 | async-start | bytes 32768 | tf_op jit(solution)/shard_map/norm/all_to_all | solution.py:281
  108.9 2.8 %convert_reduce_fusion.refs_9_ = f32[512,256]{1,0:T(8,128)S(1)} fusion(bf16[16,512,256]{2,1,0:T(8,128)(2,1)} %all-gather.2.cloned.1.call-done), kind=kLoop, calls=%fused_computation | loop fusion | flops 4063232 | bytes 4718592 | tf_op jit(solution)/shard_map/gradient/reduce_sum | solution.py:276
  111.8 3.7 %all-to-all-done.2 = f32[32,1,128]{2,1,0:T(1,128)S(1)} async-done(((f32[32,1,128]{2,1,0:T(1,128)}), f32[32,1,128]{2,1,0:T(1,128)S(1)}, u32[]{:S(2)}, u32[]{:S(2)}) %all-to-all-start.2) | async-done | bytes 16416 | tf_op jit(solution)/shard_map/norm/all_to_all | solution.py:281
  115.5 2.5 %update.1 = (bf16[512,256]{1,0:T(8,128)(2,1)}, bf16[512,256]{1,0:T(8,128)(2,1)}, bf16[512,256]{1,0:T(8,128)(2,1)}, bf16[512,256]{1,0:T(8,128)(2,1)}, bf16[512,256]{1,0:T(8,128)(2,1)}) custom-call(s32[1]{0:T(128)} %bitcast.refs_0_, s32[4,4]{1,0:T(4,128)S(1)} %copy-done.5, f32[32,128]{1,0:T(8,128)S(1)} %bitcast.28, ...), custom_call_target="tpu_custom_call" | custom-call | bytes 3424324 | tf_op jit(solution)/shard_map/update/pallas_call | solution.py:46
  (22 shorter events, 0.1 us)
Async XLA Ops:
  7.2 89.3 %all-gather.2.cloned.1.call-start = ((), (), s32[]{:S(2)}) async-start(), calls=%async_computation.3 | async-start | bytes 4456448 | tf_op jit(solution)/shard_map/outer_gather/all_gather | solution.py:255
  7.9 10.5 %collective-permute-start = (bf16[512,256]{1,0:T(8,128)(2,1)}, bf16[512,256]{1,0:T(8,128)(2,1)S(1)}, u32[]{:S(2)}, u32[]{:S(2)}) collective-permute-start(bf16[512,256]{1,0:T(8,128)(2,1)} %bitcast.24), channel_id=1, source_target_pairs={{0,0},{1,2},{2,16},{3,18},{4,4},{5,6},{6,20},{7,22},{8,8},{9,10},{... | collective-permute-start | bytes 786440 | tf_op jit(solution)/shard_map/weight_move/ppermute | solution.py:33
  19.9 34.1 %all-to-all-start = ((bf16[8,512,256]{2,1,0:T(8,128)(2,1)}), bf16[8,512,256]{2,1,0:T(8,128)(2,1)S(1)}, u32[]{:S(2)}, u32[]{:S(2)}) async-start(bf16[8,512,256]{2,1,0:T(8,128)(2,1)} %broadcast_in_dim.30), calls=%async_computation | async-start | bytes 4194304 | tf_op jit(solution)/shard_map/weight_gather/all_to_all | solution.py:236
  27.0 15.5 %collective-permute-start.1 = (bf16[128,4096]{1,0:T(8,128)(2,1)}, bf16[128,4096]{1,0:T(8,128)(2,1)}, u32[]{:S(2)}, u32[]{:S(2)}) collective-permute-start(bf16[128,4096]{1,0:T(8,128)(2,1)} %get-tuple-element.41), channel_id=1, source_target_pairs={{0,2},{2,0},{1,3},{3,1},{4,6},{6,4},{5,7},{7,5},{8,10},{10,8},{9,1... | collective-permute-start | bytes 3145736 | tf_op jit(solution)/shard_map/core_swap/ppermute | solution.py:33
  30.2 12.3 %collective-permute-start.2 = (bf16[128,4096]{1,0:T(8,128)(2,1)}, bf16[128,4096]{1,0:T(8,128)(2,1)}, u32[]{:S(2)}, u32[]{:S(2)}) collective-permute-start(bf16[128,4096]{1,0:T(8,128)(2,1)} %get-tuple-element.42), channel_id=1, source_target_pairs={{0,2},{2,0},{1,3},{3,1},{4,6},{6,4},{5,7},{7,5},{8,10},{10,8},{9,1... | collective-permute-start | bytes 3145736 | tf_op jit(solution)/shard_map/core_swap/ppermute | solution.py:33
  32.2 3.6 %collective-permute-start.3 = (f32[258,256]{1,0:T(8,128)S(1)}, f32[258,256]{1,0:T(8,128)S(1)}, u32[]{:S(2)}, u32[]{:S(2)}) collective-permute-start(f32[258,256]{1,0:T(8,128)S(1)} %pad_maximum_fusion.1), channel_id=1, source_target_pairs={{0,2},{2,0},{1,3},{3,1},{4,6},{6,4},{5,7},{7,5},{8,10},{10,8},{9,1... | collective-permute-start | bytes 792584 | tf_op jit(solution)/shard_map/core_swap/ppermute | solution.py:33
  35.8 6.7 %collective-permute-start.4 = (f32[512]{0:T(512)S(1)}, f32[512]{0:T(512)S(1)}, u32[]{:S(2)}, u32[]{:S(2)}) collective-permute-start(f32[512]{0:T(512)S(1)} %pad_maximum_fusion.2), channel_id=1, source_target_pairs={{0,1},{1,0},{2,3},{3,2},{4,5},{5,4},{6,7},{7,6},{8,9},{9,8},{10,11... | collective-permute-start | bytes 6152 | tf_op jit(solution)/shard_map/core_swap/ppermute | solution.py:33
  54.0 12.9 %copy-start.6 = (bf16[512,4096]{1,0:T(8,128)(2,1)S(1)}, bf16[512,4096]{1,0:T(8,128)(2,1)}, u32[]{:S(2)}) copy-start(bf16[512,4096]{1,0:T(8,128)(2,1)} %pad_maximum_fusion.both) | copy-start | bytes 12582916
  57.5 9.4 %collective-permute-start.5 = (bf16[512,256]{1,0:T(8,128)(2,1)S(1)}, bf16[512,256]{1,0:T(8,128)(2,1)S(1)}, u32[]{:S(2)}, u32[]{:S(2)}) collective-permute-start(bf16[512,256]{1,0:T(8,128)(2,1)S(1)} %get-tuple-element.29), channel_id=1, source_target_pairs={{0,1},{1,0},{2,3},{3,2},{4,5},{5,4},{6,7},{7,6},{8,9},{9,8},{10,11... | collective-permute-start | bytes 786440 | tf_op jit(solution)/shard_map/keys/ppermute | solution.py:33
  96.4 19.1 %copy-start = (bf16[1,512,256]{2,1,0:T(8,128)(2,1)S(1)}, bf16[1,512,256]{2,1,0:T(8,128)(2,1)}, u32[]{:S(2)}) copy-start(bf16[1,512,256]{2,1,0:T(8,128)(2,1)} %param.13) | copy-start | bytes 786436
  96.4 19.1 %copy-start.1 = (bf16[1,512,256]{2,1,0:T(8,128)(2,1)S(1)}, bf16[1,512,256]{2,1,0:T(8,128)(2,1)}, u32[]{:S(2)}) copy-start(bf16[1,512,256]{2,1,0:T(8,128)(2,1)} %param.14) | copy-start | bytes 786436
  96.4 19.1 %copy-start.2 = (bf16[1,512,256]{2,1,0:T(8,128)(2,1)S(1)}, bf16[1,512,256]{2,1,0:T(8,128)(2,1)}, u32[]{:S(2)}) copy-start(bf16[1,512,256]{2,1,0:T(8,128)(2,1)} %param.15) | copy-start | bytes 786436
  96.4 19.1 %copy-start.3 = (bf16[512,256]{1,0:T(8,128)(2,1)S(1)}, bf16[512,256]{1,0:T(8,128)(2,1)}, u32[]{:S(2)}) copy-start(bf16[512,256]{1,0:T(8,128)(2,1)} %refs_7_.1) | copy-start | bytes 786436
  96.4 19.1 %copy-start.4 = (bf16[512,256]{1,0:T(8,128)(2,1)S(1)}, bf16[512,256]{1,0:T(8,128)(2,1)}, u32[]{:S(2)}) copy-start(bf16[512,256]{1,0:T(8,128)(2,1)} %refs_8_.1) | copy-start | bytes 786436
  96.4 19.1 %copy-start.5 = (s32[4,4]{1,0:T(4,128)S(1)}, s32[4,4]{1,0:T(4,128)}, u32[]{:S(2)}) copy-start(s32[4,4]{1,0:T(4,128)} %refs_1_.1) | copy-start | bytes 196
  97.8 17.7 %collective-permute-start.6 = (bf16[512,256]{1,0:T(8,128)(2,1)}, bf16[512,256]{1,0:T(8,128)(2,1)S(1)}, u32[]{:S(2)}, u32[]{:S(2)}) collective-permute-start(bf16[512,256]{1,0:T(8,128)(2,1)} %get-tuple-element.32), channel_id=1, source_target_pairs={{0,0},{1,16},{2,1},{3,17},{4,4},{5,20},{6,5},{7,21},{8,8},{9,24},{... | collective-permute-start | bytes 786440 | tf_op jit(solution)/shard_map/gradient_home/ppermute | solution.py:33
  105.3 10.2 %all-to-all-start.2 = ((f32[32,1,128]{2,1,0:T(1,128)}), f32[32,1,128]{2,1,0:T(1,128)S(1)}, u32[]{:S(2)}, u32[]{:S(2)}) async-start(f32[32,1,128]{2,1,0:T(1,128)} %bitcast.12), calls=%async_computation.2 | async-start | bytes 32768 | tf_op jit(solution)/shard_map/norm/all_to_all | solution.py:281
Sparse Core Ops, SparseCore 0:
  10.1 75.6 all-gather.1

commit v5 on v4

--- a/solution.py
+++ b/solution.py
@@ -68,7 +68,8 @@
 
     @pl.when(step == 1)
     def _():
-        keys = (total[...] + value) * scale[...] - target[...]
+        inv = scale[...]
+        keys = jnp.where(inv == 0, 0.0, (total[...] + value) * inv) - target[...]
         part[...] = keys
         low[...] = keys.astype(BF)
 

time: 125 us -> 125 us (level)
  no operation moved by 1% of the time
where the time goes in v5:
time: 125 us
  starting transfers between devices  34.2 us (27%)
  blocking collectives  28 us (22%)
  waiting for transfers between devices  24.6 us (20%)
  between operations  14.2 us (11%)
  other arithmetic  10.5 us (8%)
  Pallas kernels  7.09 us (6%)
  local copies, waits for them, and re-layouts  4.82 us (4%)
  matrix products  1.4 us (1%)
    all_to_all x1, blocking collectives, local(): terms = lax.all_to_all(term.reshape(group, rows, cols), GROUP, 0, 0)  28 us
    ppermute x7, starting transfers between devices, permute(): return lax.ppermute(value, axes if len(axes) > 1 else axes[0], pairs)  26.5 us
    ppermute x7, waiting for transfers between devices, permute(): return lax.ppermute(value, axes if len(axes) > 1 else axes[0], pairs)  12.5 us
    all_to_all x1, waiting for transfers between devices, local(): matrix = lax.all_to_all(copies, GROUP, 0, 0).reshape(group * rows, cols)  7.62 us
    pallas_call x3, Pallas kernels, call(): pl.pallas_call(kernel, grid=grid, in_specs=in_specs, out_specs=out_specs,...  7.09 us
    all_to_all x1, starting transfers between devices, local(): matrix = lax.all_to_all(copies, GROUP, 0, 0).reshape(group * rows, cols)  4.02 us
    concatenate x1, other arithmetic, local(): both = jnp.concatenate([mine, *other], axis=0)  3.86 us
    all_to_all x1, waiting for transfers between devices, local(): partial = lax.all_to_all(partial, PLANE, 0, 0, tiled=True)  3.73 us
  transfers between devices with their start and end apart: 10, of which 6 were waited for; matrix products, arithmetic and copies ran while one was open for 13% of the time, Pallas kernels for 3%

profile of v5, /device:TPU:1, one launch (start us, length us, event | category | flops | bytes accessed | tf_op | source)
XLA Modules:
  0.0 124.8 jit_solution(7616708688570689988)
XLA Ops:
  7.2 0.0 all-gather.2.cloned.1.call-start
  7.2 0.7 all-gather.2.cloned.1.call-update
  7.9 4.6 %collective-permute-start = (bf16[512,256]{1,0:T(8,128)(2,1)}, bf16[512,256]{1,0:T(8,128)(2,1)S(1)}, u32[]{:S(2)}, u32[]{:S(2)}) collective-permute-start(bf16[512,256]{1,0:T(8,128)(2,1)} %bitcast.24), channel_id=1, source_target_pairs={{0,0},{1,2},{2,16},{3,18},{4,4},{5,6},{6,20},{7,22},{8,8},{9,10},{... | collective-permute-start | bytes 786440 | tf_op jit(solution)/shard_map/weight_move/ppermute | solution.py:33
  12.5 0.9 bitcast_convert_fusion
  13.4 0.7 compare_convert_fusion
  14.1 2.1 %multiply_reduce_fusion = f32[256]{0:T(256)S(1)} fusion(bf16[1,256,4096]{2,1,0:T(8,128)(2,1)} %param.11), kind=kLoop, calls=%fused_computation.3 | loop fusion | flops 3145472 | bytes 2098176 | tf_op jit(solution)/shard_map/core_swap/reduce_sum | solution.py:240
  16.2 2.2 %collective-permute-done = bf16[512,256]{1,0:T(8,128)(2,1)S(1)} collective-permute-done((bf16[512,256]{1,0:T(8,128)(2,1)}, bf16[512,256]{1,0:T(8,128)(2,1)S(1)}, u32[]{:S(2)}, u32[]{:S(2)}) %collective-permute-start) | collective-permute-done | bytes 262176 | tf_op jit(solution)/shard_map/weight_move/ppermute | solution.py:33
  18.4 1.5 %broadcast_in_dim.30 = bf16[8,512,256]{2,1,0:T(8,128)(2,1)} broadcast(bf16[512,256]{1,0:T(8,128)(2,1)S(1)} %collective-permute-done), dimensions={1,2} | broadcast | bytes 2359296 | tf_op jit(solution)/shard_map/weight_gather/broadcast_in_dim | solution.py:236
  19.9 4.0 %all-to-all-start = ((bf16[8,512,256]{2,1,0:T(8,128)(2,1)}), bf16[8,512,256]{2,1,0:T(8,128)(2,1)S(1)}, u32[]{:S(2)}, u32[]{:S(2)}) async-start(bf16[8,512,256]{2,1,0:T(8,128)(2,1)} %broadcast_in_dim.30), calls=%async_computation | async-start | bytes 4194304 | tf_op jit(solution)/shard_map/weight_gather/all_to_all | solution.py:237
  23.9 3.1 %fusion.1 = (bf16[128,4096]{1,0:T(8,128)(2,1)}, bf16[128,4096]{1,0:T(8,128)(2,1)}) fusion(bf16[256,4096]{1,0:T(8,128)(2,1)} %bitcast.29), kind=kLoop, calls=%fused_computation.13 | loop fusion | bytes 4194304 | tf_op jit(solution)/shard_map/core_swap/slice | solution.py:247
  27.0 3.2 %collective-permute-start.1 = (bf16[128,4096]{1,0:T(8,128)(2,1)}, bf16[128,4096]{1,0:T(8,128)(2,1)}, u32[]{:S(2)}, u32[]{:S(2)}) collective-permute-start(bf16[128,4096]{1,0:T(8,128)(2,1)} %get-tuple-element.41), channel_id=1, source_target_pairs={{0,2},{2,0},{1,3},{3,1},{4,6},{6,4},{5,7},{7,5},{8,10},{10,8},{9,1... | collective-permute-start | bytes 3145736 | tf_op jit(solution)/shard_map/core_swap/ppermute | solution.py:33
  30.2 1.9 %collective-permute-start.2 = (bf16[128,4096]{1,0:T(8,128)(2,1)}, bf16[128,4096]{1,0:T(8,128)(2,1)}, u32[]{:S(2)}, u32[]{:S(2)}) collective-permute-start(bf16[128,4096]{1,0:T(8,128)(2,1)} %get-tuple-element.42), channel_id=1, source_target_pairs={{0,2},{2,0},{1,3},{3,1},{4,6},{6,4},{5,7},{7,5},{8,10},{10,8},{9,1... | collective-permute-start | bytes 3145736 | tf_op jit(solution)/shard_map/core_swap/ppermute | solution.py:33
  32.2 2.4 %collective-permute-start.3 = (f32[258,256]{1,0:T(8,128)S(1)}, f32[258,256]{1,0:T(8,128)S(1)}, u32[]{:S(2)}, u32[]{:S(2)}) collective-permute-start(f32[258,256]{1,0:T(8,128)S(1)} %pad_maximum_fusion.1), channel_id=1, source_target_pairs={{0,2},{2,0},{1,3},{3,1},{4,6},{6,4},{5,7},{7,5},{8,10},{10,8},{9,1... | collective-permute-start | bytes 792584 | tf_op jit(solution)/shard_map/core_swap/ppermute | solution.py:33
  34.6 1.1 collective-permute-done.3
  35.8 5.0 %collective-permute-start.4 = (f32[512]{0:T(512)S(1)}, f32[512]{0:T(512)S(1)}, u32[]{:S(2)}, u32[]{:S(2)}) collective-permute-start(f32[512]{0:T(512)S(1)} %pad_maximum_fusion.2), channel_id=1, source_target_pairs={{0,1},{1,0},{2,3},{3,2},{4,5},{5,4},{6,7},{7,6},{8,9},{9,8},{10,11... | collective-permute-start | bytes 6152 | tf_op jit(solution)/shard_map/core_swap/ppermute | solution.py:33
  40.8 1.7 %collective-permute-done.4 = f32[512]{0:T(512)S(1)} collective-permute-done((f32[512]{0:T(512)S(1)}, f32[512]{0:T(512)S(1)}, u32[]{:S(2)}, u32[]{:S(2)}) %collective-permute-start.4) | collective-permute-done | bytes 2080 | tf_op jit(solution)/shard_map/core_swap/ppermute | solution.py:33
  42.6 3.9 %pad_maximum_fusion.both = bf16[512,4096]{1,0:T(8,128)(2,1)} fusion(bf16[128,4096]{1,0:T(8,128)(2,1)} %collective-permute-done.2, bf16[128,4096]{1,0:T(8,128)(2,1)} %collective-permute-done.1, bf16[256,4096]{1,0:T(8,128)(2,1)} %bitcast.30), kind=kLoop, calls=%fused_computation.2 | loop fusion | flops 12582912 | bytes 8388608 | tf_op jit(solution)/shard_map/core_swap/concatenate | solution.py:248
  46.4 7.6 %all-to-all-done = bf16[8,512,256]{2,1,0:T(8,128)(2,1)S(1)} async-done(((bf16[8,512,256]{2,1,0:T(8,128)(2,1)}), bf16[8,512,256]{2,1,0:T(8,128)(2,1)S(1)}, u32[]{:S(2)}, u32[]{:S(2)}) %all-to-all-start) | async-done | bytes 2097184 | tf_op jit(solution)/shard_map/weight_gather/all_to_all | solution.py:237
  54.0 0.1 broadcast_in_dim.32.scale
  54.2 3.4 %partial_keys.1 = (f32[512,256]{1,0:T(8,128)S(1)}, bf16[512,256]{1,0:T(8,128)(2,1)S(1)}) custom-call(bf16[512,4096]{1,0:T(8,128)(2,1)} %pad_maximum_fusion.both, bf16[4096,256]{1,0:T(8,128)(2,1)S(1)} %bitcast.23, f32[512,256]{1,0:T(8,128)S(1)} %broadcast_in_dim.32.scale, f32[512,256]{1,0:T(8,128)S(1)} %maximum_select_fusion.target), custom_call_target="tpu_custom_call" | custom-call | flops 1073741824 | bytes 8126464 | tf_op jit(solution)/shard_map/keys/partial_keys/pallas_call | solution.py:46
  57.5 1.9 %collective-permute-start.5 = (bf16[512,256]{1,0:T(8,128)(2,1)S(1)}, bf16[512,256]{1,0:T(8,128)(2,1)S(1)}, u32[]{:S(2)}, u32[]{:S(2)}) collective-permute-start(bf16[512,256]{1,0:T(8,128)(2,1)S(1)} %get-tuple-element.29), channel_id=1, source_target_pairs={{0,1},{1,0},{2,3},{3,2},{4,5},{5,4},{6,7},{7,6},{8,9},{9,8},{10,11... | collective-permute-start | bytes 786440 | tf_op jit(solution)/shard_map/keys/ppermute | solution.py:33
  59.5 7.5 %collective-permute-done.5 = bf16[512,256]{1,0:T(8,128)(2,1)S(1)} collective-permute-done((bf16[512,256]{1,0:T(8,128)(2,1)S(1)}, bf16[512,256]{1,0:T(8,128)(2,1)S(1)}, u32[]{:S(2)}, u32[]{:S(2)}) %collective-permute-start.5) | collective-permute-done | bytes 262176 | tf_op jit(solution)/shard_map/keys/ppermute | solution.py:33
  67.0 1.4 %convolution_convert_fusion = bf16[4096,256]{1,0:T(8,128)(2,1)S(1)} fusion(bf16[512,4096]{1,0:T(8,128)(2,1)S(1)} %copy-done.6, f32[512,256]{1,0:T(8,128)S(1)} %get-tuple-element.28, bf16[512,256]{1,0:T(8,128)(2,1)S(1)} %collective-permute-done.5, f32[512]{0:T(512)S(1)} %get-tuple-element.39), kind=kOutput, calls=%fused_computation.1 | convolution fusion | flops 1075314688 | bytes 7079936 | tf_op jit(solution)/shard_map/gradient/dot_general | solution.py:271
  68.4 28.0 %all_to_all.21.terms = bf16[8,512,256]{2,1,0:T(8,128)(2,1)S(1)} all-to-all(bf16[8,512,256]{2,1,0:T(8,128)(2,1)S(1)} %bitcast.31), channel_id=1, replica_groups=mesh['worker'=16,'ylo'=2,'x'=4,'core'=2,'tensor'=2] {'x','ylo'}, dimensions={0} | all-to-all | bytes 4194304 | tf_op jit(solution)/shard_map/gradient/all_to_all | solution.py:274
  96.4 0.0 copy-start.4
  96.5 0.0 all-gather.2.cloned.1.call-done
  96.5 1.3 %sum_terms.1 = (bf16[512,256]{1,0:T(8,128)(2,1)}, f32[32,128]{1,0:T(8,128)}) custom-call(bf16[8,512,256]{2,1,0:T(8,128)(2,1)S(1)} %all_to_all.21.terms), custom_call_target="tpu_custom_call" | custom-call | bytes 2375680 | tf_op jit(solution)/shard_map/gradient/sum_terms/pallas_call | solution.py:46
  97.8 7.5 %collective-permute-start.6 = (bf16[512,256]{1,0:T(8,128)(2,1)}, bf16[512,256]{1,0:T(8,128)(2,1)S(1)}, u32[]{:S(2)}, u32[]{:S(2)}) collective-permute-start(bf16[512,256]{1,0:T(8,128)(2,1)} %get-tuple-element.32), channel_id=1, source_target_pairs={{0,0},{1,16},{2,1},{3,17},{4,4},{5,20},{6,5},{7,21},{8,8},{9,24},{... | collective-permute-start | bytes 786440 | tf_op jit(solution)/shard_map/gradient_home/ppermute | solution.py:33
  105.3 3.6 %all-to-all-start.2 = ((f32[32,1,128]{2,1,0:T(1,128)}), f32[32,1,128]{2,1,0:T(1,128)S(1)}, u32[]{:S(2)}, u32[]{:S(2)}) async-start(f32[32,1,128]{2,1,0:T(1,128)} %bitcast.12), calls=%async_computation.2 | async-start | bytes 32768 | tf_op jit(solution)/shard_map/norm/all_to_all | solution.py:282
  109.0 2.8 %convert_reduce_fusion.refs_9_ = f32[512,256]{1,0:T(8,128)S(1)} fusion(bf16[16,512,256]{2,1,0:T(8,128)(2,1)} %all-gather.2.cloned.1.call-done), kind=kLoop, calls=%fused_computation | loop fusion | flops 4063232 | bytes 4718592 | tf_op jit(solution)/shard_map/gradient/reduce_sum | solution.py:277
  111.8 3.7 %all-to-all-done.2 = f32[32,1,128]{2,1,0:T(1,128)S(1)} async-done(((f32[32,1,128]{2,1,0:T(1,128)}), f32[32,1,128]{2,1,0:T(1,128)S(1)}, u32[]{:S(2)}, u32[]{:S(2)}) %all-to-all-start.2) | async-done | bytes 16416 | tf_op jit(solution)/shard_map/norm/all_to_all | solution.py:282
  115.6 2.4 %update.1 = (bf16[512,256]{1,0:T(8,128)(2,1)}, bf16[512,256]{1,0:T(8,128)(2,1)}, bf16[512,256]{1,0:T(8,128)(2,1)}, bf16[512,256]{1,0:T(8,128)(2,1)}, bf16[512,256]{1,0:T(8,128)(2,1)}) custom-call(s32[1]{0:T(128)} %bitcast.refs_0_, s32[4,4]{1,0:T(4,128)S(1)} %copy-done.5, f32[32,128]{1,0:T(8,128)S(1)} %bitcast.28, ...), custom_call_target="tpu_custom_call" | custom-call | bytes 3424324 | tf_op jit(solution)/shard_map/update/pallas_call | solution.py:46
  (22 shorter events, 0.1 us)
Async XLA Ops:
  7.2 89.3 %all-gather.2.cloned.1.call-start = ((), (), s32[]{:S(2)}) async-start(), calls=%async_computation.3 | async-start | bytes 4456448 | tf_op jit(solution)/shard_map/outer_gather/all_gather | solution.py:256
  7.9 10.5 %collective-permute-start = (bf16[512,256]{1,0:T(8,128)(2,1)}, bf16[512,256]{1,0:T(8,128)(2,1)S(1)}, u32[]{:S(2)}, u32[]{:S(2)}) collective-permute-start(bf16[512,256]{1,0:T(8,128)(2,1)} %bitcast.24), channel_id=1, source_target_pairs={{0,0},{1,2},{2,16},{3,18},{4,4},{5,6},{6,20},{7,22},{8,8},{9,10},{... | collective-permute-start | bytes 786440 | tf_op jit(solution)/shard_map/weight_move/ppermute | solution.py:33
  19.9 34.1 %all-to-all-start = ((bf16[8,512,256]{2,1,0:T(8,128)(2,1)}), bf16[8,512,256]{2,1,0:T(8,128)(2,1)S(1)}, u32[]{:S(2)}, u32[]{:S(2)}) async-start(bf16[8,512,256]{2,1,0:T(8,128)(2,1)} %broadcast_in_dim.30), calls=%async_computation | async-start | bytes 4194304 | tf_op jit(solution)/shard_map/weight_gather/all_to_all | solution.py:237
  27.0 15.5 %collective-permute-start.1 = (bf16[128,4096]{1,0:T(8,128)(2,1)}, bf16[128,4096]{1,0:T(8,128)(2,1)}, u32[]{:S(2)}, u32[]{:S(2)}) collective-permute-start(bf16[128,4096]{1,0:T(8,128)(2,1)} %get-tuple-element.41), channel_id=1, source_target_pairs={{0,2},{2,0},{1,3},{3,1},{4,6},{6,4},{5,7},{7,5},{8,10},{10,8},{9,1... | collective-permute-start | bytes 3145736 | tf_op jit(solution)/shard_map/core_swap/ppermute | solution.py:33
  30.2 12.3 %collective-permute-start.2 = (bf16[128,4096]{1,0:T(8,128)(2,1)}, bf16[128,4096]{1,0:T(8,128)(2,1)}, u32[]{:S(2)}, u32[]{:S(2)}) collective-permute-start(bf16[128,4096]{1,0:T(8,128)(2,1)} %get-tuple-element.42), channel_id=1, source_target_pairs={{0,2},{2,0},{1,3},{3,1},{4,6},{6,4},{5,7},{7,5},{8,10},{10,8},{9,1... | collective-permute-start | bytes 3145736 | tf_op jit(solution)/shard_map/core_swap/ppermute | solution.py:33
  32.2 3.6 %collective-permute-start.3 = (f32[258,256]{1,0:T(8,128)S(1)}, f32[258,256]{1,0:T(8,128)S(1)}, u32[]{:S(2)}, u32[]{:S(2)}) collective-permute-start(f32[258,256]{1,0:T(8,128)S(1)} %pad_maximum_fusion.1), channel_id=1, source_target_pairs={{0,2},{2,0},{1,3},{3,1},{4,6},{6,4},{5,7},{7,5},{8,10},{10,8},{9,1... | collective-permute-start | bytes 792584 | tf_op jit(solution)/shard_map/core_swap/ppermute | solution.py:33
  35.8 6.7 %collective-permute-start.4 = (f32[512]{0:T(512)S(1)}, f32[512]{0:T(512)S(1)}, u32[]{:S(2)}, u32[]{:S(2)}) collective-permute-start(f32[512]{0:T(512)S(1)} %pad_maximum_fusion.2), channel_id=1, source_target_pairs={{0,1},{1,0},{2,3},{3,2},{4,5},{5,4},{6,7},{7,6},{8,9},{9,8},{10,11... | collective-permute-start | bytes 6152 | tf_op jit(solution)/shard_map/core_swap/ppermute | solution.py:33
  54.0 12.9 %copy-start.6 = (bf16[512,4096]{1,0:T(8,128)(2,1)S(1)}, bf16[512,4096]{1,0:T(8,128)(2,1)}, u32[]{:S(2)}) copy-start(bf16[512,4096]{1,0:T(8,128)(2,1)} %pad_maximum_fusion.both) | copy-start | bytes 12582916
  57.5 9.4 %collective-permute-start.5 = (bf16[512,256]{1,0:T(8,128)(2,1)S(1)}, bf16[512,256]{1,0:T(8,128)(2,1)S(1)}, u32[]{:S(2)}, u32[]{:S(2)}) collective-permute-start(bf16[512,256]{1,0:T(8,128)(2,1)S(1)} %get-tuple-element.29), channel_id=1, source_target_pairs={{0,1},{1,0},{2,3},{3,2},{4,5},{5,4},{6,7},{7,6},{8,9},{9,8},{10,11... | collective-permute-start | bytes 786440 | tf_op jit(solution)/shard_map/keys/ppermute | solution.py:33
  96.4 19.1 %copy-start = (bf16[1,512,256]{2,1,0:T(8,128)(2,1)S(1)}, bf16[1,512,256]{2,1,0:T(8,128)(2,1)}, u32[]{:S(2)}) copy-start(bf16[1,512,256]{2,1,0:T(8,128)(2,1)} %param.13) | copy-start | bytes 786436
  96.4 19.1 %copy-start.1 = (bf16[1,512,256]{2,1,0:T(8,128)(2,1)S(1)}, bf16[1,512,256]{2,1,0:T(8,128)(2,1)}, u32[]{:S(2)}) copy-start(bf16[1,512,256]{2,1,0:T(8,128)(2,1)} %param.14) | copy-start | bytes 786436
  96.4 19.1 %copy-start.2 = (bf16[1,512,256]{2,1,0:T(8,128)(2,1)S(1)}, bf16[1,512,256]{2,1,0:T(8,128)(2,1)}, u32[]{:S(2)}) copy-start(bf16[1,512,256]{2,1,0:T(8,128)(2,1)} %param.15) | copy-start | bytes 786436
  96.4 19.1 %copy-start.3 = (bf16[512,256]{1,0:T(8,128)(2,1)S(1)}, bf16[512,256]{1,0:T(8,128)(2,1)}, u32[]{:S(2)}) copy-start(bf16[512,256]{1,0:T(8,128)(2,1)} %refs_7_.1) | copy-start | bytes 786436
  96.4 19.1 %copy-start.4 = (bf16[512,256]{1,0:T(8,128)(2,1)S(1)}, bf16[512,256]{1,0:T(8,128)(2,1)}, u32[]{:S(2)}) copy-start(bf16[512,256]{1,0:T(8,128)(2,1)} %refs_8_.1) | copy-start | bytes 786436
  96.4 19.1 %copy-start.5 = (s32[4,4]{1,0:T(4,128)S(1)}, s32[4,4]{1,0:T(4,128)}, u32[]{:S(2)}) copy-start(s32[4,4]{1,0:T(4,128)} %refs_1_.1) | copy-start | bytes 196
  97.8 17.7 %collective-permute-start.6 = (bf16[512,256]{1,0:T(8,128)(2,1)}, bf16[512,256]{1,0:T(8,128)(2,1)S(1)}, u32[]{:S(2)}, u32[]{:S(2)}) collective-permute-start(bf16[512,256]{1,0:T(8,128)(2,1)} %get-tuple-element.32), channel_id=1, source_target_pairs={{0,0},{1,16},{2,1},{3,17},{4,4},{5,20},{6,5},{7,21},{8,8},{9,24},{... | collective-permute-start | bytes 786440 | tf_op jit(solution)/shard_map/gradient_home/ppermute | solution.py:33
  105.3 10.2 %all-to-all-start.2 = ((f32[32,1,128]{2,1,0:T(1,128)}), f32[32,1,128]{2,1,0:T(1,128)S(1)}, u32[]{:S(2)}, u32[]{:S(2)}) async-start(f32[32,1,128]{2,1,0:T(1,128)} %bitcast.12), calls=%async_computation.2 | async-start | bytes 32768 | tf_op jit(solution)/shard_map/norm/all_to_all | solution.py:282
Sparse Core Ops, SparseCore 0:
  10.1 75.6 all-gather.1

commit v6 on v5

--- a/solution.py
+++ b/solution.py
@@ -58,7 +58,7 @@
     )(*ins)
 
 
-def keys_kernel(both, matrix, scale, target, part, low, total):
+def keys_kernel(both, matrix, scale, target, low, total):
     step = pl.program_id(0)
     value = jnp.dot(both[...], matrix[...], preferred_element_type=F32)
 
@@ -69,8 +69,8 @@
     @pl.when(step == 1)
     def _():
         inv = scale[...]
-        keys = jnp.where(inv == 0, 0.0, (total[...] + value) * inv) - target[...]
-        part[...] = keys
+        keys = jnp.where(inv == 0, 0.0, (total[...] + value) * inv)
+        keys -= target[...].astype(F32)
         low[...] = keys.astype(BF)
 
 
@@ -79,7 +79,6 @@
     cols = matrix.shape[1]
     depth = half // 2
     outs = [
-        jax.ShapeDtypeStruct((tokens, cols), F32),
         jax.ShapeDtypeStruct((tokens, cols), BF),
     ]
     full = pl.BlockSpec((tokens, cols), lambda k: (0, 0))
@@ -95,7 +94,7 @@
             full,
         ],
         outs,
-        [full, full],
+        [full],
         [pltpu.VMEM((tokens, cols), F32)],
         2 * tokens * half * cols,
         48 * 2**20,
@@ -258,14 +257,14 @@
     with jax.named_scope("keys"):
         shape = (2 * tokens, cols)
         spread = jnp.broadcast_to(inv2[:, None], shape)
-        shift = jnp.where(core == side, target2, 0.0)
+        shift = jnp.where(core == side, target2, 0.0).astype(BF)
         both, spread, shift, matrix = lax.optimization_barrier(
             (both, spread, shift, matrix)
         )
-        part, low = partial_keys(both, matrix, spread, shift)
-        theirs = swap(low, "tensor")
+        (part,) = partial_keys(both, matrix, spread, shift)
+        theirs = swap(part, "tensor")
         scale = (inv2 * mask2)[:, None]
-        resid = ((part + theirs.astype(F32)) * scale).astype(BF)
+        resid = ((part.astype(F32) + theirs.astype(F32)) * scale).astype(BF)
 
     with jax.named_scope("gradient"):
         term = lax.dot_general(

time: 125 us -> 126 us (level)
  no operation moved by 1% of the time
where the time goes in v6:
time: 126 us; the launch traced here: 125 us
  starting transfers between devices  34.2 us (27%)
  blocking collectives  28.1 us (22%)
  waiting for transfers between devices  24.5 us (19%)
  between operations  14.2 us (11%)
  other arithmetic  10.6 us (8%)
  Pallas kernels  7.11 us (6%)
  local copies, waits for them, and re-layouts  4.81 us (4%)
  matrix products  1.39 us (1%)
    all_to_all x1, blocking collectives, local(): terms = lax.all_to_all(term.reshape(group, rows, cols), GROUP, 0, 0)  28.1 us
    ppermute x7, starting transfers between devices, permute(): return lax.ppermute(value, axes if len(axes) > 1 else axes[0], pairs)  26.5 us
    ppermute x7, waiting for transfers between devices, permute(): return lax.ppermute(value, axes if len(axes) > 1 else axes[0], pairs)  12.5 us
    all_to_all x1, waiting for transfers between devices, local(): matrix = lax.all_to_all(copies, GROUP, 0, 0).reshape(group * rows, cols)  7.52 us
    pallas_call x3, Pallas kernels, call(): pl.pallas_call(kernel, grid=grid, in_specs=in_specs, out_specs=out_specs,...  7.11 us
    all_to_all x1, starting transfers between devices, local(): matrix = lax.all_to_all(copies, GROUP, 0, 0).reshape(group * rows, cols)  4.02 us
    concatenate x1, other arithmetic, local(): both = jnp.concatenate([mine, *other], axis=0)  3.96 us
    all_to_all x1, waiting for transfers between devices, local(): partial = lax.all_to_all(partial, PLANE, 0, 0, tiled=True)  3.73 us
  transfers between devices with their start and end apart: 10, of which 6 were waited for; matrix products, arithmetic and copies ran while one was open for 13% of the time, Pallas kernels for 3%

profile of v6, /device:TPU:1, one launch (start us, length us, event | category | flops | bytes accessed | tf_op | source)
XLA Modules:
  0.0 124.9 jit_solution(9969262136331110047)
XLA Ops:
  7.2 0.0 all-gather.2.cloned.1.call-start
  7.2 0.7 all-gather.2.cloned.1.call-update
  7.9 4.6 %collective-permute-start = (bf16[512,256]{1,0:T(8,128)(2,1)}, bf16[512,256]{1,0:T(8,128)(2,1)S(1)}, u32[]{:S(2)}, u32[]{:S(2)}) collective-permute-start(bf16[512,256]{1,0:T(8,128)(2,1)} %bitcast.24), channel_id=1, source_target_pairs={{0,0},{1,2},{2,16},{3,18},{4,4},{5,6},{6,20},{7,22},{8,8},{9,10},{... | collective-permute-start | bytes 786440 | tf_op jit(solution)/shard_map/weight_move/ppermute | solution.py:33
  12.5 0.9 bitcast_convert_fusion
  13.4 0.7 compare_convert_fusion
  14.1 2.1 %multiply_reduce_fusion = f32[256]{0:T(256)S(1)} fusion(bf16[1,256,4096]{2,1,0:T(8,128)(2,1)} %param.11), kind=kLoop, calls=%fused_computation.3 | loop fusion | flops 3145472 | bytes 2098176 | tf_op jit(solution)/shard_map/core_swap/reduce_sum | solution.py:239
  16.2 2.2 %collective-permute-done = bf16[512,256]{1,0:T(8,128)(2,1)S(1)} collective-permute-done((bf16[512,256]{1,0:T(8,128)(2,1)}, bf16[512,256]{1,0:T(8,128)(2,1)S(1)}, u32[]{:S(2)}, u32[]{:S(2)}) %collective-permute-start) | collective-permute-done | bytes 262176 | tf_op jit(solution)/shard_map/weight_move/ppermute | solution.py:33
  18.4 1.5 %broadcast_in_dim.30 = bf16[8,512,256]{2,1,0:T(8,128)(2,1)} broadcast(bf16[512,256]{1,0:T(8,128)(2,1)S(1)} %collective-permute-done), dimensions={1,2} | broadcast | bytes 2359296 | tf_op jit(solution)/shard_map/weight_gather/broadcast_in_dim | solution.py:235
  19.9 4.0 %all-to-all-start = ((bf16[8,512,256]{2,1,0:T(8,128)(2,1)}), bf16[8,512,256]{2,1,0:T(8,128)(2,1)S(1)}, u32[]{:S(2)}, u32[]{:S(2)}) async-start(bf16[8,512,256]{2,1,0:T(8,128)(2,1)} %broadcast_in_dim.30), calls=%async_computation | async-start | bytes 4194304 | tf_op jit(solution)/shard_map/weight_gather/all_to_all | solution.py:236
  23.9 3.1 %fusion.2 = (bf16[128,4096]{1,0:T(8,128)(2,1)}, bf16[128,4096]{1,0:T(8,128)(2,1)}) fusion(bf16[256,4096]{1,0:T(8,128)(2,1)} %bitcast.29), kind=kLoop, calls=%fused_computation.14 | loop fusion | bytes 4194304 | tf_op jit(solution)/shard_map/core_swap/slice | solution.py:246
  27.0 3.2 %collective-permute-start.1 = (bf16[128,4096]{1,0:T(8,128)(2,1)}, bf16[128,4096]{1,0:T(8,128)(2,1)}, u32[]{:S(2)}, u32[]{:S(2)}) collective-permute-start(bf16[128,4096]{1,0:T(8,128)(2,1)} %get-tuple-element.37), channel_id=1, source_target_pairs={{0,2},{2,0},{1,3},{3,1},{4,6},{6,4},{5,7},{7,5},{8,10},{10,8},{9,1... | collective-permute-start | bytes 3145736 | tf_op jit(solution)/shard_map/core_swap/ppermute | solution.py:33
  30.2 1.9 %collective-permute-start.2 = (bf16[128,4096]{1,0:T(8,128)(2,1)}, bf16[128,4096]{1,0:T(8,128)(2,1)}, u32[]{:S(2)}, u32[]{:S(2)}) collective-permute-start(bf16[128,4096]{1,0:T(8,128)(2,1)} %get-tuple-element.38), channel_id=1, source_target_pairs={{0,2},{2,0},{1,3},{3,1},{4,6},{6,4},{5,7},{7,5},{8,10},{10,8},{9,1... | collective-permute-start | bytes 3145736 | tf_op jit(solution)/shard_map/core_swap/ppermute | solution.py:33
  32.2 2.4 %collective-permute-start.3 = (f32[258,256]{1,0:T(8,128)S(1)}, f32[258,256]{1,0:T(8,128)S(1)}, u32[]{:S(2)}, u32[]{:S(2)}) collective-permute-start(f32[258,256]{1,0:T(8,128)S(1)} %pad_maximum_fusion.1), channel_id=1, source_target_pairs={{0,2},{2,0},{1,3},{3,1},{4,6},{6,4},{5,7},{7,5},{8,10},{10,8},{9,1... | collective-permute-start | bytes 792584 | tf_op jit(solution)/shard_map/core_swap/ppermute | solution.py:33
  34.6 1.1 collective-permute-done.3
  35.8 5.0 %collective-permute-start.4 = (f32[512]{0:T(512)S(1)}, f32[512]{0:T(512)S(1)}, u32[]{:S(2)}, u32[]{:S(2)}) collective-permute-start(f32[512]{0:T(512)S(1)} %pad_maximum_fusion.2), channel_id=1, source_target_pairs={{0,1},{1,0},{2,3},{3,2},{4,5},{5,4},{6,7},{7,6},{8,9},{9,8},{10,11... | collective-permute-start | bytes 6152 | tf_op jit(solution)/shard_map/core_swap/ppermute | solution.py:33
  40.8 0.1 fusion.target
  40.8 1.7 %collective-permute-done.4 = f32[512]{0:T(512)S(1)} collective-permute-done((f32[512]{0:T(512)S(1)}, f32[512]{0:T(512)S(1)}, u32[]{:S(2)}, u32[]{:S(2)}) %collective-permute-start.4) | collective-permute-done | bytes 2080 | tf_op jit(solution)/shard_map/core_swap/ppermute | solution.py:33
  42.5 4.0 %pad_maximum_fusion.both = bf16[512,4096]{1,0:T(8,128)(2,1)} fusion(bf16[128,4096]{1,0:T(8,128)(2,1)} %collective-permute-done.2, bf16[128,4096]{1,0:T(8,128)(2,1)} %collective-permute-done.1, bf16[256,4096]{1,0:T(8,128)(2,1)} %bitcast.30), kind=kLoop, calls=%fused_computation.2 | loop fusion | flops 12582912 | bytes 8388608 | tf_op jit(solution)/shard_map/core_swap/concatenate | solution.py:247
  46.5 7.5 %all-to-all-done = bf16[8,512,256]{2,1,0:T(8,128)(2,1)S(1)} async-done(((bf16[8,512,256]{2,1,0:T(8,128)(2,1)}), bf16[8,512,256]{2,1,0:T(8,128)(2,1)S(1)}, u32[]{:S(2)}, u32[]{:S(2)}) %all-to-all-start) | async-done | bytes 2097184 | tf_op jit(solution)/shard_map/weight_gather/all_to_all | solution.py:236
  54.0 0.1 broadcast_in_dim.32.scale
  54.2 3.4 %partial_keys.1 = bf16[512,256]{1,0:T(8,128)(2,1)S(1)} custom-call(bf16[512,4096]{1,0:T(8,128)(2,1)} %pad_maximum_fusion.both, bf16[4096,256]{1,0:T(8,128)(2,1)S(1)} %bitcast.23, f32[512,256]{1,0:T(8,128)S(1)} %broadcast_in_dim.32.scale, bf16[512,256]{1,0:T(8,128)(2,1)S(1)} %fusion.target), custom_call_target="tpu_custom_call" | custom-call | flops 1073741824 | bytes 7340032 | tf_op jit(solution)/shard_map/keys/partial_keys/pallas_call | solution.py:46
  57.5 1.9 %collective-permute-start.5 = (bf16[512,256]{1,0:T(8,128)(2,1)S(1)}, bf16[512,256]{1,0:T(8,128)(2,1)S(1)}, u32[]{:S(2)}, u32[]{:S(2)}) collective-permute-start(bf16[512,256]{1,0:T(8,128)(2,1)S(1)} %partial_keys.1), channel_id=1, source_target_pairs={{0,1},{1,0},{2,3},{3,2},{4,5},{5,4},{6,7},{7,6},{8,9},{9,8},{10,11... | collective-permute-start | bytes 786440 | tf_op jit(solution)/shard_map/keys/ppermute | solution.py:33
  59.5 7.5 %collective-permute-done.5 = bf16[512,256]{1,0:T(8,128)(2,1)S(1)} collective-permute-done((bf16[512,256]{1,0:T(8,128)(2,1)S(1)}, bf16[512,256]{1,0:T(8,128)(2,1)S(1)}, u32[]{:S(2)}, u32[]{:S(2)}) %collective-permute-start.5) | collective-permute-done | bytes 262176 | tf_op jit(solution)/shard_map/keys/ppermute | solution.py:33
  67.0 1.4 %convolution_convert_fusion = bf16[4096,256]{1,0:T(8,128)(2,1)S(1)} fusion(bf16[512,4096]{1,0:T(8,128)(2,1)S(1)} %copy-done.6, bf16[512,256]{1,0:T(8,128)(2,1)S(1)} %collective-permute-done.5, bf16[512,256]{1,0:T(8,128)(2,1)S(1)} %partial_keys.1, f32[512]{0:T(512)S(1)} %get-tuple-element.35), kind=kOutput, calls=%fused_computation.1 | convolution fusion | flops 1075445760 | bytes 6817792 | tf_op jit(solution)/shard_map/gradient/dot_general | solution.py:270
  68.4 28.1 %all_to_all.21.terms = bf16[8,512,256]{2,1,0:T(8,128)(2,1)S(1)} all-to-all(bf16[8,512,256]{2,1,0:T(8,128)(2,1)S(1)} %bitcast.31), channel_id=1, replica_groups=mesh['worker'=16,'ylo'=2,'x'=4,'core'=2,'tensor'=2] {'x','ylo'}, dimensions={0} | all-to-all | bytes 4194304 | tf_op jit(solution)/shard_map/gradient/all_to_all | solution.py:273
  96.5 0.0 all-gather.2.cloned.1.call-done
  96.6 1.3 %sum_terms.1 = (bf16[512,256]{1,0:T(8,128)(2,1)}, f32[32,128]{1,0:T(8,128)}) custom-call(bf16[8,512,256]{2,1,0:T(8,128)(2,1)S(1)} %all_to_all.21.terms), custom_call_target="tpu_custom_call" | custom-call | bytes 2375680 | tf_op jit(solution)/shard_map/gradient/sum_terms/pallas_call | solution.py:46
  97.9 7.5 %collective-permute-start.6 = (bf16[512,256]{1,0:T(8,128)(2,1)}, bf16[512,256]{1,0:T(8,128)(2,1)S(1)}, u32[]{:S(2)}, u32[]{:S(2)}) collective-permute-start(bf16[512,256]{1,0:T(8,128)(2,1)} %get-tuple-element.28), channel_id=1, source_target_pairs={{0,0},{1,16},{2,1},{3,17},{4,4},{5,20},{6,5},{7,21},{8,8},{9,24},{... | collective-permute-start | bytes 786440 | tf_op jit(solution)/shard_map/gradient_home/ppermute | solution.py:33
  105.4 3.6 %all-to-all-start.2 = ((f32[32,1,128]{2,1,0:T(1,128)}), f32[32,1,128]{2,1,0:T(1,128)S(1)}, u32[]{:S(2)}, u32[]{:S(2)}) async-start(f32[32,1,128]{2,1,0:T(1,128)} %bitcast.12), calls=%async_computation.2 | async-start | bytes 32768 | tf_op jit(solution)/shard_map/norm/all_to_all | solution.py:281
  109.0 2.8 %convert_reduce_fusion.refs_9_ = f32[512,256]{1,0:T(8,128)S(1)} fusion(bf16[16,512,256]{2,1,0:T(8,128)(2,1)} %all-gather.2.cloned.1.call-done), kind=kLoop, calls=%fused_computation | loop fusion | flops 4063232 | bytes 4718592 | tf_op jit(solution)/shard_map/gradient/reduce_sum | solution.py:276
  111.9 3.7 %all-to-all-done.2 = f32[32,1,128]{2,1,0:T(1,128)S(1)} async-done(((f32[32,1,128]{2,1,0:T(1,128)}), f32[32,1,128]{2,1,0:T(1,128)S(1)}, u32[]{:S(2)}, u32[]{:S(2)}) %all-to-all-start.2) | async-done | bytes 16416 | tf_op jit(solution)/shard_map/norm/all_to_all | solution.py:281
  115.7 2.4 %update.1 = (bf16[512,256]{1,0:T(8,128)(2,1)}, bf16[512,256]{1,0:T(8,128)(2,1)}, bf16[512,256]{1,0:T(8,128)(2,1)}, bf16[512,256]{1,0:T(8,128)(2,1)}, bf16[512,256]{1,0:T(8,128)(2,1)}) custom-call(s32[1]{0:T(128)} %bitcast.refs_0_, s32[4,4]{1,0:T(4,128)S(1)} %copy-done.5, f32[32,128]{1,0:T(8,128)S(1)} %bitcast.28, ...), custom_call_target="tpu_custom_call" | custom-call | bytes 3424324 | tf_op jit(solution)/shard_map/update/pallas_call | solution.py:46
  (22 shorter events, 0.1 us)
Async XLA Ops:
  7.2 89.4 %all-gather.2.cloned.1.call-start = ((), (), s32[]{:S(2)}) async-start(), calls=%async_computation.3 | async-start | bytes 4456448 | tf_op jit(solution)/shard_map/outer_gather/all_gather | solution.py:255
  7.9 10.5 %collective-permute-start = (bf16[512,256]{1,0:T(8,128)(2,1)}, bf16[512,256]{1,0:T(8,128)(2,1)S(1)}, u32[]{:S(2)}, u32[]{:S(2)}) collective-permute-start(bf16[512,256]{1,0:T(8,128)(2,1)} %bitcast.24), channel_id=1, source_target_pairs={{0,0},{1,2},{2,16},{3,18},{4,4},{5,6},{6,20},{7,22},{8,8},{9,10},{... | collective-permute-start | bytes 786440 | tf_op jit(solution)/shard_map/weight_move/ppermute | solution.py:33
  19.9 34.1 %all-to-all-start = ((bf16[8,512,256]{2,1,0:T(8,128)(2,1)}), bf16[8,512,256]{2,1,0:T(8,128)(2,1)S(1)}, u32[]{:S(2)}, u32[]{:S(2)}) async-start(bf16[8,512,256]{2,1,0:T(8,128)(2,1)} %broadcast_in_dim.30), calls=%async_computation | async-start | bytes 4194304 | tf_op jit(solution)/shard_map/weight_gather/all_to_all | solution.py:236
  27.0 15.5 %collective-permute-start.1 = (bf16[128,4096]{1,0:T(8,128)(2,1)}, bf16[128,4096]{1,0:T(8,128)(2,1)}, u32[]{:S(2)}, u32[]{:S(2)}) collective-permute-start(bf16[128,4096]{1,0:T(8,128)(2,1)} %get-tuple-element.37), channel_id=1, source_target_pairs={{0,2},{2,0},{1,3},{3,1},{4,6},{6,4},{5,7},{7,5},{8,10},{10,8},{9,1... | collective-permute-start | bytes 3145736 | tf_op jit(solution)/shard_map/core_swap/ppermute | solution.py:33
  30.2 12.3 %collective-permute-start.2 = (bf16[128,4096]{1,0:T(8,128)(2,1)}, bf16[128,4096]{1,0:T(8,128)(2,1)}, u32[]{:S(2)}, u32[]{:S(2)}) collective-permute-start(bf16[128,4096]{1,0:T(8,128)(2,1)} %get-tuple-element.38), channel_id=1, source_target_pairs={{0,2},{2,0},{1,3},{3,1},{4,6},{6,4},{5,7},{7,5},{8,10},{10,8},{9,1... | collective-permute-start | bytes 3145736 | tf_op jit(solution)/shard_map/core_swap/ppermute | solution.py:33
  32.2 3.6 %collective-permute-start.3 = (f32[258,256]{1,0:T(8,128)S(1)}, f32[258,256]{1,0:T(8,128)S(1)}, u32[]{:S(2)}, u32[]{:S(2)}) collective-permute-start(f32[258,256]{1,0:T(8,128)S(1)} %pad_maximum_fusion.1), channel_id=1, source_target_pairs={{0,2},{2,0},{1,3},{3,1},{4,6},{6,4},{5,7},{7,5},{8,10},{10,8},{9,1... | collective-permute-start | bytes 792584 | tf_op jit(solution)/shard_map/core_swap/ppermute | solution.py:33
  35.8 6.7 %collective-permute-start.4 = (f32[512]{0:T(512)S(1)}, f32[512]{0:T(512)S(1)}, u32[]{:S(2)}, u32[]{:S(2)}) collective-permute-start(f32[512]{0:T(512)S(1)} %pad_maximum_fusion.2), channel_id=1, source_target_pairs={{0,1},{1,0},{2,3},{3,2},{4,5},{5,4},{6,7},{7,6},{8,9},{9,8},{10,11... | collective-permute-start | bytes 6152 | tf_op jit(solution)/shard_map/core_swap/ppermute | solution.py:33
  54.0 12.9 %copy-start.6 = (bf16[512,4096]{1,0:T(8,128)(2,1)S(1)}, bf16[512,4096]{1,0:T(8,128)(2,1)}, u32[]{:S(2)}) copy-start(bf16[512,4096]{1,0:T(8,128)(2,1)} %pad_maximum_fusion.both) | copy-start | bytes 12582916
  57.5 9.4 %collective-permute-start.5 = (bf16[512,256]{1,0:T(8,128)(2,1)S(1)}, bf16[512,256]{1,0:T(8,128)(2,1)S(1)}, u32[]{:S(2)}, u32[]{:S(2)}) collective-permute-start(bf16[512,256]{1,0:T(8,128)(2,1)S(1)} %partial_keys.1), channel_id=1, source_target_pairs={{0,1},{1,0},{2,3},{3,2},{4,5},{5,4},{6,7},{7,6},{8,9},{9,8},{10,11... | collective-permute-start | bytes 786440 | tf_op jit(solution)/shard_map/keys/ppermute | solution.py:33
  96.5 19.1 %copy-start = (bf16[1,512,256]{2,1,0:T(8,128)(2,1)S(1)}, bf16[1,512,256]{2,1,0:T(8,128)(2,1)}, u32[]{:S(2)}) copy-start(bf16[1,512,256]{2,1,0:T(8,128)(2,1)} %param.13) | copy-start | bytes 786436
  96.5 19.1 %copy-start.1 = (bf16[1,512,256]{2,1,0:T(8,128)(2,1)S(1)}, bf16[1,512,256]{2,1,0:T(8,128)(2,1)}, u32[]{:S(2)}) copy-start(bf16[1,512,256]{2,1,0:T(8,128)(2,1)} %param.14) | copy-start | bytes 786436
  96.5 19.1 %copy-start.2 = (bf16[1,512,256]{2,1,0:T(8,128)(2,1)S(1)}, bf16[1,512,256]{2,1,0:T(8,128)(2,1)}, u32[]{:S(2)}) copy-start(bf16[1,512,256]{2,1,0:T(8,128)(2,1)} %param.15) | copy-start | bytes 786436
  96.5 19.1 %copy-start.3 = (bf16[512,256]{1,0:T(8,128)(2,1)S(1)}, bf16[512,256]{1,0:T(8,128)(2,1)}, u32[]{:S(2)}) copy-start(bf16[512,256]{1,0:T(8,128)(2,1)} %refs_7_.1) | copy-start | bytes 786436
  96.5 19.1 %copy-start.4 = (bf16[512,256]{1,0:T(8,128)(2,1)S(1)}, bf16[512,256]{1,0:T(8,128)(2,1)}, u32[]{:S(2)}) copy-start(bf16[512,256]{1,0:T(8,128)(2,1)} %refs_8_.1) | copy-start | bytes 786436
  96.5 19.1 %copy-start.5 = (s32[4,4]{1,0:T(4,128)S(1)}, s32[4,4]{1,0:T(4,128)}, u32[]{:S(2)}) copy-start(s32[4,4]{1,0:T(4,128)} %refs_1_.1) | copy-start | bytes 196
  97.9 17.7 %collective-permute-start.6 = (bf16[512,256]{1,0:T(8,128)(2,1)}, bf16[512,256]{1,0:T(8,128)(2,1)S(1)}, u32[]{:S(2)}, u32[]{:S(2)}) collective-permute-start(bf16[512,256]{1,0:T(8,128)(2,1)} %get-tuple-element.28), channel_id=1, source_target_pairs={{0,0},{1,16},{2,1},{3,17},{4,4},{5,20},{6,5},{7,21},{8,8},{9,24},{... | collective-permute-start | bytes 786440 | tf_op jit(solution)/shard_map/gradient_home/ppermute | solution.py:33
  105.4 10.2 %all-to-all-start.2 = ((f32[32,1,128]{2,1,0:T(1,128)}), f32[32,1,128]{2,1,0:T(1,128)S(1)}, u32[]{:S(2)}, u32[]{:S(2)}) async-start(f32[32,1,128]{2,1,0:T(1,128)} %bitcast.12), calls=%async_computation.2 | async-start | bytes 32768 | tf_op jit(solution)/shard_map/norm/all_to_all | solution.py:281
Sparse Core Ops, SparseCore 0:
  10.1 75.8 all-gather.1
